TPU v7x, 512 devices: a whole 4x4x16 slice. The times are simulated.
512 devices in a mesh: dp: 4 (over x), ctx: 16 (over z), tp: 8 (over y, core).
Axes of the slice: x: 4, y: 4, z: 16, core: 2. Of those that a mesh axis runs over, the one named last changes fastest.
Arguments:
- conv_input: bfloat16 [4, 4096, 10240], P('dp', 'ctx', 'tp'), may hold values from -6 to 6
- step_raw: float32 [4, 4096, 128], P('dp', 'ctx', 'tp'), may hold values from -3 to 3
- doc_starts: int32 [4, 4096], P('dp', 'ctx'), may hold values 0 or 1
- decay_power: int32 [128], P('tp'), may hold values from 0 to 3
- conv_weight: bfloat16 [4, 10240], P(None, 'tp'), may hold values from -3 to 3
- conv_bias: float32 [10240], P('tp'), may hold values from -3 to 3
- step_bias: float32 [128], P('tp'), may hold values from -7.3 to -2.25
- skip_gain: float32 [128], P('tp'), may hold values from 0.1 to 4
- grad_out: bfloat16 [4, 4096, 8192], P('dp', 'ctx', 'tp'), may hold values from -6 to 6
Outputs:
- grad_input: bfloat16 [4, 4096, 10240], P('dp', 'ctx', 'tp')
- grad_step_raw: float32 [4, 4096, 128], P('dp', 'ctx', 'tp')
- grad_conv_weight: float32 [4, 8, 1280], P(None, 'tp', ('dp', 'ctx'))
- grad_conv_bias: float32 [8, 1280], P('tp', ('dp', 'ctx'))
All inputs are finite; a program needn't handle non-finite values. No bound on the sum of `doc_starts` on one device may be relied on, other than what follows from the above.
Results may differ from a plain program's by a relative error of at most 0.017.
Values may be sent and summed in bfloat16 or wider, within the bound.
No kernel may reach another device: no remote copies, remote signals or barrier semaphores. Data moves between devices by JAX's collectives and lax.ppermute only.
A program may use at most 128 MiB of HBM per device.

v0:
```python
import math

import jax
import jax.numpy as jnp
from jax import lax
from jax.sharding import PartitionSpec as P

BLOCK = 128
HEAD_WIDTH = 64
STATE = 128
KERNEL = 4


def shifted(value, axis, by):
    devices = lax.axis_size(axis)
    pairs = [(i, i + by) for i in range(devices) if 0 <= i + by < devices]
    return lax.ppermute(value, axis, pairs)


def decay_rates(decay_power, length):
    return -0.5 * jnp.exp((decay_power.astype(jnp.float32) / 3.0 - 1.0) * math.log(length))


def conv_activate(padded, weight32, bias):
    count = padded.shape[0] - (KERNEL - 1)
    total = bias[None, :] + padded[0:count] * weight32[0][None, :]
    for offset in range(1, KERNEL):
        total = total + padded[offset : offset + count] * weight32[offset][None, :]
    return jax.nn.silu(total).astype(jnp.bfloat16)


def split_channels(activated, heads):
    count = activated.shape[0]
    inner = heads * HEAD_WIDTH
    values = activated[:, :inner].reshape(count, heads, HEAD_WIDTH)
    keys = activated[:, inner : inner + STATE]
    queries = activated[:, inner + STATE : inner + 2 * STATE]
    return (values, keys, queries)


def block_prefix(decay_log, starts_block):
    cumulative = jnp.cumsum(decay_log, axis=0)
    doc_index = jnp.cumsum(starts_block)
    alive = (doc_index == 0.0).astype(jnp.float32)
    return (cumulative, doc_index, alive)


def block_state(state, values, keys, step_size, cumulative, doc_index, alive):
    tail = (
        jnp.exp(cumulative[-1][None, :] - cumulative)
        * (doc_index == doc_index[-1]).astype(jnp.float32)[:, None]
    )
    weighted = (values.astype(jnp.float32) * (step_size * tail)[:, :, None]).astype(jnp.bfloat16)
    fresh = jnp.einsum("shp,sn->hpn", weighted, keys, preferred_element_type=jnp.float32)
    return fresh + (jnp.exp(cumulative[-1]) * alive[-1])[:, None, None] * state


def block_step(state, pieces, skip_gain):
    activated, step_size, decay_log, starts_block = pieces
    heads = step_size.shape[1]
    count = activated.shape[0]
    values, keys, queries = split_channels(activated, heads)
    cumulative, doc_index, alive = block_prefix(decay_log, starts_block)
    positions = jnp.arange(count)
    lower = (
        (positions[:, None] >= positions[None, :]) & (doc_index[:, None] == doc_index[None, :])
    ).astype(jnp.float32)
    across = cumulative.T
    gaps = jnp.minimum(across[:, :, None] - across[:, None, :], 0.0)
    scores = jnp.dot(queries, keys.T, preferred_element_type=jnp.float32)
    mixing = (scores[None] * jnp.exp(gaps) * lower[None] * step_size.T[:, None, :]).astype(
        jnp.bfloat16
    )
    local = jnp.einsum("hts,shp->thp", mixing, values, preferred_element_type=jnp.float32)
    carried = jnp.einsum(
        "tn,hpn->thp", queries.astype(jnp.float32), state, precision=lax.Precision.HIGHEST
    )
    out_decay = jnp.exp(cumulative) * alive[:, None]
    result = (
        local
        + out_decay[:, :, None] * carried
        + skip_gain[None, :, None] * values.astype(jnp.float32)
    )
    following = block_state(state, values, keys, step_size, cumulative, doc_index, alive)
    return (following, result.reshape(count, heads * HEAD_WIDTH))


def block_pieces(activated, step_size, decay_log, flags):
    blocks = activated.shape[0] // BLOCK
    return (
        activated.reshape(blocks, BLOCK, activated.shape[1]),
        step_size.reshape(blocks, BLOCK, step_size.shape[1]),
        decay_log.reshape(blocks, BLOCK, decay_log.shape[1]),
        flags.reshape(blocks, BLOCK),
    )


def run_blocks(state, activated, step_size, decay_log, flags, skip_gain):
    count = activated.shape[0]
    pieces = block_pieces(activated, step_size, decay_log, flags)
    final, outputs = lax.scan(lambda carry, item: block_step(carry, item, skip_gain), state, pieces)
    return (outputs.reshape(count, outputs.shape[2]), final)


def body(
    conv_input,
    step_raw,
    doc_starts,
    decay_power,
    conv_weight,
    conv_bias,
    step_bias,
    skip_gain,
    grad_out,
):
    tokens = conv_input.shape[1]
    heads = step_raw.shape[2]
    inner = heads * HEAD_WIDTH
    ctx_size = lax.axis_size("ctx")
    seq_len = tokens * ctx_size
    rates = decay_rates(decay_power, seq_len)
    flags = doc_starts[0].astype(jnp.float32)
    rim = shifted(conv_input[0, tokens - (KERNEL - 1) :], "ctx", 1)
    padded = jnp.concatenate([rim, conv_input[0]], 0).astype(jnp.float32)
    weight32 = conv_weight.astype(jnp.float32)
    activated, conv_pull = jax.vjp(conv_activate, padded, weight32, conv_bias)
    step_size, step_pull = jax.vjp(
        lambda raw: jax.nn.softplus(raw + step_bias[None, :]), step_raw[0]
    )
    decay_log = step_size * rates[None, :]
    zeros = jnp.zeros((heads, HEAD_WIDTH, STATE), jnp.float32)

    def state_only(carry, item):
        act_block, step_block, log_block, start_block = item
        values, keys, queries = split_channels(act_block, heads)
        cumulative, doc_index, alive = block_prefix(log_block, start_block)
        return (block_state(carry, values, keys, step_block, cumulative, doc_index, alive), None)

    fresh, _ = lax.scan(state_only, zeros, block_pieces(activated, step_size, decay_log, flags))
    passing = jnp.exp(jnp.sum(decay_log, axis=0)) * (jnp.sum(flags) == 0.0).astype(jnp.float32)
    cotangent = grad_out[0].astype(jnp.float32)
    reach = (
        jnp.exp(jnp.cumsum(decay_log, axis=0))
        * (jnp.cumsum(flags) == 0.0).astype(jnp.float32)[:, None]
    )
    weighted_grad = cotangent.reshape(tokens, heads, HEAD_WIDTH) * reach[:, :, None]
    local_grad = jnp.einsum(
        "thp,tn->hpn",
        weighted_grad,
        activated[:, inner + STATE :].astype(jnp.float32),
        precision=lax.Precision.HIGHEST,
    )

    def turn(step, carry):
        entering_now, later_now = carry
        sent_up = shifted(passing[:, None, None] * entering_now + fresh, "ctx", 1)
        sent_down = shifted(passing[:, None, None] * later_now + local_grad, "ctx", -1)
        return (sent_up, sent_down)

    entering, later = lax.fori_loop(0, ctx_size - 1, turn, (zeros, zeros))

    def segment(state, act_in, step_in):
        return run_blocks(state, act_in, step_in, step_in * rates[None, :], flags, skip_gain)

    _, segment_pull = jax.vjp(segment, entering, activated, step_size)
    _, grad_act, grad_step = segment_pull((cotangent, later))
    grad_padded, grad_weight, grad_bias = conv_pull(grad_act)
    (grad_raw,) = step_pull(grad_step)
    back = shifted(grad_padded[: KERNEL - 1], "ctx", -1)
    edge = tokens - (KERNEL - 1)
    grad_tail = grad_padded[KERNEL - 1 :]
    grad_input = jnp.concatenate([grad_tail[:edge], grad_tail[edge:] + back], 0).astype(
        jnp.bfloat16
    )
    term = jnp.concatenate([grad_weight, grad_bias[None, :]], 0)
    shard = lax.psum_scatter(term, ("dp", "ctx"), scatter_dimension=1, tiled=True)
    scale = 1.0 / (lax.axis_size("dp") * seq_len)
    shard = shard * scale
    return (grad_input[None], grad_raw[None], shard[:KERNEL][:, None, :], shard[KERNEL][None, :])


def solution(mesh):
    return jax.shard_map(
        body,
        mesh=mesh,
        in_specs=(
            P("dp", "ctx", "tp"),
            P("dp", "ctx", "tp"),
            P("dp", "ctx"),
            P("tp"),
            P(None, "tp"),
            P("tp"),
            P("tp"),
            P("tp"),
            P("dp", "ctx", "tp"),
        ),
        out_specs=(
            P("dp", "ctx", "tp"),
            P("dp", "ctx", "tp"),
            P(None, "tp", ("dp", "ctx")),
            P("tp", ("dp", "ctx")),
        ),
        check_vma=False,
    )
```

profile of v0, /device:TPU:24, one launch (start us, length us, event | category | flops | bytes accessed | tf_op | source)
XLA Modules:
  0.0 702.9 jit_solution(997878800354399362)
XLA Ops:
  24.3 11.2 %while.110 = (s32[]{:T(128)}, f32[16,64,128]{2,1,0:T(8,128)S(1)}, bf16[2,128,1280]{2,1,0:T(8,128)(2,1)}, f32[2,128,16]{2,1,0:T(8,128)}, f32[2,128,16]{2,1,0:T(8,...) while((s32[]{:T(128)}, f32[16,64,128]{2,1,0:T(8,128)S(1)}, ...), condition=%wide.region_5.6_spmd.clone, body=%wide.region_2.5_spmd.clone.sunk | while | flops 34623636 | bytes 4183517 | solution.py:139
  37.5 276.3 %while.107 = (s32[]{:T(128)}, f32[16,64,128]{2,1,0:T(8,128)S(1)}, f32[16,64,128]{2,1,0:T(8,128)S(1)}, f32[16]{0:T(128)S(1)}, f32[16,64,128]{2,1,0:T(8,128)S(1)}, /*index=5*/f32[16,64,128]{2,1,0:T(8,128)S(1)}, s32[]{:T(128)}) while((s32[]{:T(128)}, f32[16,64,128]{2,1,0:T(8,128)S(1)}, f32[16,64,128]{2,1,0:T(8,128)S(1)}, f32[16]{0:T(128)S(1)}, ...), condition=%wide.region_11.12_spmd, body=%wide.region_10.11_spmd.sunk | while | flops 524290 | bytes 7340253 | solution.py:160
  43.9 9.9 %collective-permute-done = f32[16,64,128]{2,1,0:T(8,128)S(1)} collective-permute-done((f32[16,64,128]{2,1,0:T(8,128)}, f32[16,64,128]{2,1,0:T(8,128)S(1)}, u32[]{:S(2)}, u32[]{:S(2)}) %collective-permute-start) | collective-permute-done | bytes 524320 | tf_op jit(solution)/shard_map/while/body/eval_jaxpr/ppermute | solution.py:17
  59.2 5.0 collective-permute-start
  65.6 8.9 %collective-permute-done = f32[16,64,128]{2,1,0:T(8,128)S(1)} collective-permute-done((f32[16,64,128]{2,1,0:T(8,128)}, f32[16,64,128]{2,1,0:T(8,128)S(1)}, u32[]{:S(2)}, u32[]{:S(2)}) %collective-permute-start) | collective-permute-done | bytes 524320 | tf_op jit(solution)/shard_map/while/body/eval_jaxpr/ppermute | solution.py:17
  79.8 4.7 collective-permute-start
  85.8 7.7 %collective-permute-done = f32[16,64,128]{2,1,0:T(8,128)S(1)} collective-permute-done((f32[16,64,128]{2,1,0:T(8,128)}, f32[16,64,128]{2,1,0:T(8,128)S(1)}, u32[]{:S(2)}, u32[]{:S(2)}) %collective-permute-start) | collective-permute-done | bytes 524320 | tf_op jit(solution)/shard_map/while/body/eval_jaxpr/ppermute | solution.py:17
  98.8 4.7 collective-permute-start
  104.8 7.0 collective-permute-done
  122.6 5.7 collective-permute-done
  128.2 4.3 collective-permute-done.1
  138.7 5.7 collective-permute-done
  144.4 4.3 collective-permute-done.1
  155.0 5.7 collective-permute-done
  160.7 4.3 collective-permute-done.1
  170.9 5.8 collective-permute-done
  176.7 4.6 collective-permute-done.1
  187.6 7.2 %collective-permute-done = f32[16,64,128]{2,1,0:T(8,128)S(1)} collective-permute-done((f32[16,64,128]{2,1,0:T(8,128)}, f32[16,64,128]{2,1,0:T(8,128)S(1)}, u32[]{:S(2)}, u32[]{:S(2)}) %collective-permute-start) | collective-permute-done | bytes 524320 | tf_op jit(solution)/shard_map/while/body/eval_jaxpr/ppermute | solution.py:17
  194.7 4.6 collective-permute-done.1
  205.5 8.5 %collective-permute-done = f32[16,64,128]{2,1,0:T(8,128)S(1)} collective-permute-done((f32[16,64,128]{2,1,0:T(8,128)}, f32[16,64,128]{2,1,0:T(8,128)S(1)}, u32[]{:S(2)}, u32[]{:S(2)}) %collective-permute-start) | collective-permute-done | bytes 524320 | tf_op jit(solution)/shard_map/while/body/eval_jaxpr/ppermute | solution.py:17
  214.0 4.6 collective-permute-done.1
  223.2 9.5 %collective-permute-done = f32[16,64,128]{2,1,0:T(8,128)S(1)} collective-permute-done((f32[16,64,128]{2,1,0:T(8,128)}, f32[16,64,128]{2,1,0:T(8,128)S(1)}, u32[]{:S(2)}, u32[]{:S(2)}) %collective-permute-start) | collective-permute-done | bytes 524320 | tf_op jit(solution)/shard_map/while/body/eval_jaxpr/ppermute | solution.py:17
  232.7 4.5 collective-permute-done.1
  244.0 11.1 %collective-permute-done = f32[16,64,128]{2,1,0:T(8,128)S(1)} collective-permute-done((f32[16,64,128]{2,1,0:T(8,128)}, f32[16,64,128]{2,1,0:T(8,128)S(1)}, u32[]{:S(2)}, u32[]{:S(2)}) %collective-permute-start) | collective-permute-done | bytes 524320 | tf_op jit(solution)/shard_map/while/body/eval_jaxpr/ppermute | solution.py:17
  255.1 4.4 collective-permute-done.1
  264.7 10.4 %collective-permute-done = f32[16,64,128]{2,1,0:T(8,128)S(1)} collective-permute-done((f32[16,64,128]{2,1,0:T(8,128)}, f32[16,64,128]{2,1,0:T(8,128)S(1)}, u32[]{:S(2)}, u32[]{:S(2)}) %collective-permute-start) | collective-permute-done | bytes 524320 | tf_op jit(solution)/shard_map/while/body/eval_jaxpr/ppermute | solution.py:17
  284.4 9.3 %collective-permute-done = f32[16,64,128]{2,1,0:T(8,128)S(1)} collective-permute-done((f32[16,64,128]{2,1,0:T(8,128)}, f32[16,64,128]{2,1,0:T(8,128)S(1)}, u32[]{:S(2)}, u32[]{:S(2)}) %collective-permute-start) | collective-permute-done | bytes 524320 | tf_op jit(solution)/shard_map/while/body/eval_jaxpr/ppermute | solution.py:17
  303.9 5.7 collective-permute-done
  309.6 4.3 collective-permute-done.1
  313.9 62.8 %while.109 = (s32[]{:T(128)}, f32[16,64,128]{2,1,0:T(8,128)S(1)}, f32[2,16,128,128]{3,2,1,0:T(8,128)}, bf16[2,128,128]{1,2,0:T(8,128)(2,1)}, bf16[2,128,128]{2,1...) while((s32[]{:T(128)}, f32[16,64,128]{2,1,0:T(8,128)S(1)}, ...), condition=%wide.region_15.16_spmd.clone.clone, body=%wide.region_12.15_spmd.clone.clone.sunk | while | flops 244368288 | bytes 15097273 | solution.py:101
  378.8 34.7 %while.108 = (s32[]{:T(128)}, f32[16,64,128]{2,1,0:T(8,128)S(1)}, bf16[2,128,1280]{2,1,0:T(8,128)(2,1)}, f32[2,128,16]{1,0,2:T(2,128)}, f32[2,128,16]{2,1,0:T(8,...) while((s32[]{:T(128)}, f32[16,64,128]{2,1,0:T(8,128)S(1)}, ...), condition=%wide.region_26.27_spmd, body=%wide.region_16.26_spmd.sunk | while | flops 551798784 | bytes 38757704 | solution.py:101
  418.5 275.6 %all-reduce.13 = f32[5,1280]{1,0:T(8,128)S(1)} all-reduce(f32[5,1280]{1,0:T(8,128)S(1)} %pad_maximum_fusion.1), channel_id=2, replica_groups=mesh['dp'=4,'ctx'=16,'tp'=8] {'dp','ctx'}, use_global_device_ids=true, to_apply=%region_32.33.clone | all-reduce | flops 6400 | bytes 51200
  (539 shorter events, 249.3 us)
Async XLA Ops:
  1.4 20.6 %collective-permute-start.2 = (bf16[3,1280]{1,0:T(4,128)(2,1)S(1)}, bf16[3,1280]{1,0:T(4,128)(2,1)S(1)}, u32[]{:S(2)}, u32[]{:S(2)}) collective-permute-start(bf16[3,1280]{1,0:T(4,128)(2,1)S(1)} %slice_bitcast_fusion.6), channel_id=1, source_target_pairs={{0,8},{8,16},{16,24},{24,32},{32,40},{40,48},{48,56},{56,64},{64,7... | collective-permute-start | bytes 23048 | tf_op jit(solution)/shard_map/ppermute | solution.py:17
  38.8 15.0 %collective-permute-start = (f32[16,64,128]{2,1,0:T(8,128)}, f32[16,64,128]{2,1,0:T(8,128)S(1)}, u32[]{:S(2)}, u32[]{:S(2)}) collective-permute-start(f32[16,64,128]{2,1,0:T(8,128)} %get-tuple-element.1989), channel_id=1, source_target_pairs={{0,8},{8,16},{16,24},{24,32},{32,40},{40,48},{48,56},{56,64},{64,7... | collective-permute-start | bytes 1572872 | tf_op jit(solution)/shard_map/while/body/eval_jaxpr/ppermute | solution.py:17
  42.6 15.4 %collective-permute-start.1 = (f32[16,64,128]{2,1,0:T(8,128)}, f32[16,64,128]{2,1,0:T(8,128)S(1)}, u32[]{:S(2)}, u32[]{:S(2)}) collective-permute-start(f32[16,64,128]{2,1,0:T(8,128)} %get-tuple-element.1990), channel_id=1, source_target_pairs={{8,0},{16,8},{24,16},{32,24},{40,32},{48,40},{56,48},{64,56},{72,6... | collective-permute-start | bytes 1572872 | tf_op jit(solution)/shard_map/while/body/eval_jaxpr/ppermute | solution.py:17
  59.2 15.3 %collective-permute-start = (f32[16,64,128]{2,1,0:T(8,128)}, f32[16,64,128]{2,1,0:T(8,128)S(1)}, u32[]{:S(2)}, u32[]{:S(2)}) collective-permute-start(f32[16,64,128]{2,1,0:T(8,128)} %get-tuple-element.1989), channel_id=1, source_target_pairs={{0,8},{8,16},{16,24},{24,32},{32,40},{40,48},{48,56},{56,64},{64,7... | collective-permute-start | bytes 1572872 | tf_op jit(solution)/shard_map/while/body/eval_jaxpr/ppermute | solution.py:17
  64.3 14.3 %collective-permute-start.1 = (f32[16,64,128]{2,1,0:T(8,128)}, f32[16,64,128]{2,1,0:T(8,128)S(1)}, u32[]{:S(2)}, u32[]{:S(2)}) collective-permute-start(f32[16,64,128]{2,1,0:T(8,128)} %get-tuple-element.1990), channel_id=1, source_target_pairs={{8,0},{16,8},{24,16},{32,24},{40,32},{48,40},{56,48},{64,56},{72,6... | collective-permute-start | bytes 1572872 | tf_op jit(solution)/shard_map/while/body/eval_jaxpr/ppermute | solution.py:17
  79.8 13.7 %collective-permute-start = (f32[16,64,128]{2,1,0:T(8,128)}, f32[16,64,128]{2,1,0:T(8,128)S(1)}, u32[]{:S(2)}, u32[]{:S(2)}) collective-permute-start(f32[16,64,128]{2,1,0:T(8,128)} %get-tuple-element.1989), channel_id=1, source_target_pairs={{0,8},{8,16},{16,24},{24,32},{32,40},{40,48},{48,56},{56,64},{64,7... | collective-permute-start | bytes 1572872 | tf_op jit(solution)/shard_map/while/body/eval_jaxpr/ppermute | solution.py:17
  84.5 13.1 %collective-permute-start.1 = (f32[16,64,128]{2,1,0:T(8,128)}, f32[16,64,128]{2,1,0:T(8,128)S(1)}, u32[]{:S(2)}, u32[]{:S(2)}) collective-permute-start(f32[16,64,128]{2,1,0:T(8,128)} %get-tuple-element.1990), channel_id=1, source_target_pairs={{8,0},{16,8},{24,16},{32,24},{40,32},{48,40},{56,48},{64,56},{72,6... | collective-permute-start | bytes 1572872 | tf_op jit(solution)/shard_map/while/body/eval_jaxpr/ppermute | solution.py:17
  98.8 13.0 %collective-permute-start = (f32[16,64,128]{2,1,0:T(8,128)}, f32[16,64,128]{2,1,0:T(8,128)S(1)}, u32[]{:S(2)}, u32[]{:S(2)}) collective-permute-start(f32[16,64,128]{2,1,0:T(8,128)} %get-tuple-element.1989), channel_id=1, source_target_pairs={{0,8},{8,16},{16,24},{24,32},{32,40},{40,48},{48,56},{56,64},{64,7... | collective-permute-start | bytes 1572872 | tf_op jit(solution)/shard_map/while/body/eval_jaxpr/ppermute | solution.py:17
  103.5 12.4 %collective-permute-start.1 = (f32[16,64,128]{2,1,0:T(8,128)}, f32[16,64,128]{2,1,0:T(8,128)S(1)}, u32[]{:S(2)}, u32[]{:S(2)}) collective-permute-start(f32[16,64,128]{2,1,0:T(8,128)} %get-tuple-element.1990), channel_id=1, source_target_pairs={{8,0},{16,8},{24,16},{32,24},{40,32},{48,40},{56,48},{64,56},{72,6... | collective-permute-start | bytes 1572872 | tf_op jit(solution)/shard_map/while/body/eval_jaxpr/ppermute | solution.py:17
  117.1 11.2 %collective-permute-start = (f32[16,64,128]{2,1,0:T(8,128)}, f32[16,64,128]{2,1,0:T(8,128)S(1)}, u32[]{:S(2)}, u32[]{:S(2)}) collective-permute-start(f32[16,64,128]{2,1,0:T(8,128)} %get-tuple-element.1989), channel_id=1, source_target_pairs={{0,8},{8,16},{16,24},{24,32},{32,40},{40,48},{48,56},{56,64},{64,7... | collective-permute-start | bytes 1572872 | tf_op jit(solution)/shard_map/while/body/eval_jaxpr/ppermute | solution.py:17
  121.3 11.3 %collective-permute-start.1 = (f32[16,64,128]{2,1,0:T(8,128)}, f32[16,64,128]{2,1,0:T(8,128)S(1)}, u32[]{:S(2)}, u32[]{:S(2)}) collective-permute-start(f32[16,64,128]{2,1,0:T(8,128)} %get-tuple-element.1990), channel_id=1, source_target_pairs={{8,0},{16,8},{24,16},{32,24},{40,32},{48,40},{56,48},{64,56},{72,6... | collective-permute-start | bytes 1572872 | tf_op jit(solution)/shard_map/while/body/eval_jaxpr/ppermute | solution.py:17
  133.8 10.6 %collective-permute-start = (f32[16,64,128]{2,1,0:T(8,128)}, f32[16,64,128]{2,1,0:T(8,128)S(1)}, u32[]{:S(2)}, u32[]{:S(2)}) collective-permute-start(f32[16,64,128]{2,1,0:T(8,128)} %get-tuple-element.1989), channel_id=1, source_target_pairs={{0,8},{8,16},{16,24},{24,32},{32,40},{40,48},{48,56},{56,64},{64,7... | collective-permute-start | bytes 1572872 | tf_op jit(solution)/shard_map/while/body/eval_jaxpr/ppermute | solution.py:17
  137.4 11.3 %collective-permute-start.1 = (f32[16,64,128]{2,1,0:T(8,128)}, f32[16,64,128]{2,1,0:T(8,128)S(1)}, u32[]{:S(2)}, u32[]{:S(2)}) collective-permute-start(f32[16,64,128]{2,1,0:T(8,128)} %get-tuple-element.1990), channel_id=1, source_target_pairs={{8,0},{16,8},{24,16},{32,24},{40,32},{48,40},{56,48},{64,56},{72,6... | collective-permute-start | bytes 1572872 | tf_op jit(solution)/shard_map/while/body/eval_jaxpr/ppermute | solution.py:17
  149.9 10.8 %collective-permute-start = (f32[16,64,128]{2,1,0:T(8,128)}, f32[16,64,128]{2,1,0:T(8,128)S(1)}, u32[]{:S(2)}, u32[]{:S(2)}) collective-permute-start(f32[16,64,128]{2,1,0:T(8,128)} %get-tuple-element.1989), channel_id=1, source_target_pairs={{0,8},{8,16},{16,24},{24,32},{32,40},{40,48},{48,56},{56,64},{64,7... | collective-permute-start | bytes 1572872 | tf_op jit(solution)/shard_map/while/body/eval_jaxpr/ppermute | solution.py:17
  153.7 11.3 %collective-permute-start.1 = (f32[16,64,128]{2,1,0:T(8,128)}, f32[16,64,128]{2,1,0:T(8,128)S(1)}, u32[]{:S(2)}, u32[]{:S(2)}) collective-permute-start(f32[16,64,128]{2,1,0:T(8,128)} %get-tuple-element.1990), channel_id=1, source_target_pairs={{8,0},{16,8},{24,16},{32,24},{40,32},{48,40},{56,48},{64,56},{72,6... | collective-permute-start | bytes 1572872 | tf_op jit(solution)/shard_map/while/body/eval_jaxpr/ppermute | solution.py:17
  166.2 10.5 %collective-permute-start = (f32[16,64,128]{2,1,0:T(8,128)}, f32[16,64,128]{2,1,0:T(8,128)S(1)}, u32[]{:S(2)}, u32[]{:S(2)}) collective-permute-start(f32[16,64,128]{2,1,0:T(8,128)} %get-tuple-element.1989), channel_id=1, source_target_pairs={{0,8},{8,16},{16,24},{24,32},{32,40},{40,48},{48,56},{56,64},{64,7... | collective-permute-start | bytes 1572872 | tf_op jit(solution)/shard_map/while/body/eval_jaxpr/ppermute | solution.py:17
  169.6 11.7 %collective-permute-start.1 = (f32[16,64,128]{2,1,0:T(8,128)}, f32[16,64,128]{2,1,0:T(8,128)S(1)}, u32[]{:S(2)}, u32[]{:S(2)}) collective-permute-start(f32[16,64,128]{2,1,0:T(8,128)} %get-tuple-element.1990), channel_id=1, source_target_pairs={{8,0},{16,8},{24,16},{32,24},{40,32},{48,40},{56,48},{64,56},{72,6... | collective-permute-start | bytes 1572872 | tf_op jit(solution)/shard_map/while/body/eval_jaxpr/ppermute | solution.py:17
  182.5 12.2 %collective-permute-start = (f32[16,64,128]{2,1,0:T(8,128)}, f32[16,64,128]{2,1,0:T(8,128)S(1)}, u32[]{:S(2)}, u32[]{:S(2)}) collective-permute-start(f32[16,64,128]{2,1,0:T(8,128)} %get-tuple-element.1989), channel_id=1, source_target_pairs={{0,8},{8,16},{16,24},{24,32},{32,40},{40,48},{48,56},{56,64},{64,7... | collective-permute-start | bytes 1572872 | tf_op jit(solution)/shard_map/while/body/eval_jaxpr/ppermute | solution.py:17
  186.2 13.1 %collective-permute-start.1 = (f32[16,64,128]{2,1,0:T(8,128)}, f32[16,64,128]{2,1,0:T(8,128)S(1)}, u32[]{:S(2)}, u32[]{:S(2)}) collective-permute-start(f32[16,64,128]{2,1,0:T(8,128)} %get-tuple-element.1990), channel_id=1, source_target_pairs={{8,0},{16,8},{24,16},{32,24},{40,32},{48,40},{56,48},{64,56},{72,6... | collective-permute-start | bytes 1572872 | tf_op jit(solution)/shard_map/while/body/eval_jaxpr/ppermute | solution.py:17
  200.5 13.5 %collective-permute-start = (f32[16,64,128]{2,1,0:T(8,128)}, f32[16,64,128]{2,1,0:T(8,128)S(1)}, u32[]{:S(2)}, u32[]{:S(2)}) collective-permute-start(f32[16,64,128]{2,1,0:T(8,128)} %get-tuple-element.1989), channel_id=1, source_target_pairs={{0,8},{8,16},{16,24},{24,32},{32,40},{40,48},{48,56},{56,64},{64,7... | collective-permute-start | bytes 1572872 | tf_op jit(solution)/shard_map/while/body/eval_jaxpr/ppermute | solution.py:17
  204.2 14.4 %collective-permute-start.1 = (f32[16,64,128]{2,1,0:T(8,128)}, f32[16,64,128]{2,1,0:T(8,128)S(1)}, u32[]{:S(2)}, u32[]{:S(2)}) collective-permute-start(f32[16,64,128]{2,1,0:T(8,128)} %get-tuple-element.1990), channel_id=1, source_target_pairs={{8,0},{16,8},{24,16},{32,24},{40,32},{48,40},{56,48},{64,56},{72,6... | collective-permute-start | bytes 1572872 | tf_op jit(solution)/shard_map/while/body/eval_jaxpr/ppermute | solution.py:17
  219.8 12.9 %collective-permute-start = (f32[16,64,128]{2,1,0:T(8,128)}, f32[16,64,128]{2,1,0:T(8,128)S(1)}, u32[]{:S(2)}, u32[]{:S(2)}) collective-permute-start(f32[16,64,128]{2,1,0:T(8,128)} %get-tuple-element.1989), channel_id=1, source_target_pairs={{0,8},{8,16},{16,24},{24,32},{32,40},{40,48},{48,56},{56,64},{64,7... | collective-permute-start | bytes 1572872 | tf_op jit(solution)/shard_map/while/body/eval_jaxpr/ppermute | solution.py:17
  221.9 15.3 %collective-permute-start.1 = (f32[16,64,128]{2,1,0:T(8,128)}, f32[16,64,128]{2,1,0:T(8,128)S(1)}, u32[]{:S(2)}, u32[]{:S(2)}) collective-permute-start(f32[16,64,128]{2,1,0:T(8,128)} %get-tuple-element.1990), channel_id=1, source_target_pairs={{8,0},{16,8},{24,16},{32,24},{40,32},{48,40},{56,48},{64,56},{72,6... | collective-permute-start | bytes 1572872 | tf_op jit(solution)/shard_map/while/body/eval_jaxpr/ppermute | solution.py:17
  238.4 16.6 %collective-permute-start = (f32[16,64,128]{2,1,0:T(8,128)}, f32[16,64,128]{2,1,0:T(8,128)S(1)}, u32[]{:S(2)}, u32[]{:S(2)}) collective-permute-start(f32[16,64,128]{2,1,0:T(8,128)} %get-tuple-element.1989), channel_id=1, source_target_pairs={{0,8},{8,16},{16,24},{24,32},{32,40},{40,48},{48,56},{56,64},{64,7... | collective-permute-start | bytes 1572872 | tf_op jit(solution)/shard_map/while/body/eval_jaxpr/ppermute | solution.py:17
  242.7 16.8 %collective-permute-start.1 = (f32[16,64,128]{2,1,0:T(8,128)}, f32[16,64,128]{2,1,0:T(8,128)S(1)}, u32[]{:S(2)}, u32[]{:S(2)}) collective-permute-start(f32[16,64,128]{2,1,0:T(8,128)} %get-tuple-element.1990), channel_id=1, source_target_pairs={{8,0},{16,8},{24,16},{32,24},{40,32},{48,40},{56,48},{64,56},{72,6... | collective-permute-start | bytes 1572872 | tf_op jit(solution)/shard_map/while/body/eval_jaxpr/ppermute | solution.py:17
  260.7 14.4 %collective-permute-start = (f32[16,64,128]{2,1,0:T(8,128)}, f32[16,64,128]{2,1,0:T(8,128)S(1)}, u32[]{:S(2)}, u32[]{:S(2)}) collective-permute-start(f32[16,64,128]{2,1,0:T(8,128)} %get-tuple-element.1989), channel_id=1, source_target_pairs={{0,8},{8,16},{16,24},{24,32},{32,40},{40,48},{48,56},{56,64},{64,7... | collective-permute-start | bytes 1572872 | tf_op jit(solution)/shard_map/while/body/eval_jaxpr/ppermute | solution.py:17
  263.4 15.8 %collective-permute-start.1 = (f32[16,64,128]{2,1,0:T(8,128)}, f32[16,64,128]{2,1,0:T(8,128)S(1)}, u32[]{:S(2)}, u32[]{:S(2)}) collective-permute-start(f32[16,64,128]{2,1,0:T(8,128)} %get-tuple-element.1990), channel_id=1, source_target_pairs={{8,0},{16,8},{24,16},{32,24},{40,32},{48,40},{56,48},{64,56},{72,6... | collective-permute-start | bytes 1572872 | tf_op jit(solution)/shard_map/while/body/eval_jaxpr/ppermute | solution.py:17
  280.4 13.3 %collective-permute-start = (f32[16,64,128]{2,1,0:T(8,128)}, f32[16,64,128]{2,1,0:T(8,128)S(1)}, u32[]{:S(2)}, u32[]{:S(2)}) collective-permute-start(f32[16,64,128]{2,1,0:T(8,128)} %get-tuple-element.1989), channel_id=1, source_target_pairs={{0,8},{8,16},{16,24},{24,32},{32,40},{40,48},{48,56},{56,64},{64,7... | collective-permute-start | bytes 1572872 | tf_op jit(solution)/shard_map/while/body/eval_jaxpr/ppermute | solution.py:17
  283.1 14.7 %collective-permute-start.1 = (f32[16,64,128]{2,1,0:T(8,128)}, f32[16,64,128]{2,1,0:T(8,128)S(1)}, u32[]{:S(2)}, u32[]{:S(2)}) collective-permute-start(f32[16,64,128]{2,1,0:T(8,128)} %get-tuple-element.1990), channel_id=1, source_target_pairs={{8,0},{16,8},{24,16},{32,24},{40,32},{48,40},{56,48},{64,56},{72,6... | collective-permute-start | bytes 1572872 | tf_op jit(solution)/shard_map/while/body/eval_jaxpr/ppermute | solution.py:17
  298.9 10.6 %collective-permute-start = (f32[16,64,128]{2,1,0:T(8,128)}, f32[16,64,128]{2,1,0:T(8,128)S(1)}, u32[]{:S(2)}, u32[]{:S(2)}) collective-permute-start(f32[16,64,128]{2,1,0:T(8,128)} %get-tuple-element.1989), channel_id=1, source_target_pairs={{0,8},{8,16},{16,24},{24,32},{32,40},{40,48},{48,56},{56,64},{64,7... | collective-permute-start | bytes 1572872 | tf_op jit(solution)/shard_map/while/body/eval_jaxpr/ppermute | solution.py:17
  302.6 11.3 %collective-permute-start.1 = (f32[16,64,128]{2,1,0:T(8,128)}, f32[16,64,128]{2,1,0:T(8,128)S(1)}, u32[]{:S(2)}, u32[]{:S(2)}) collective-permute-start(f32[16,64,128]{2,1,0:T(8,128)} %get-tuple-element.1990), channel_id=1, source_target_pairs={{8,0},{16,8},{24,16},{32,24},{40,32},{48,40},{56,48},{64,56},{72,6... | collective-permute-start | bytes 1572872 | tf_op jit(solution)/shard_map/while/body/eval_jaxpr/ppermute | solution.py:17
  695.6 5.7 collective-permute-start.3
  (106 other events, 1742.9 us)
where the time goes:
time: 706 us; the launch traced here: 703 us
  blocking collectives  276 us (39%)
  waiting for transfers between devices  185 us (26%)
  starting transfers between devices  80.4 us (11%)
  other arithmetic  76.8 us (11%)
  local copies, waits for them, and re-layouts  57.9 us (8%)
  matrix products  21.7 us (3%)
    unnamed x1, blocking collectives  276 us
    ppermute x32, waiting for transfers between devices, shifted(): return lax.ppermute(value, axis, pairs)  185 us
    ppermute x32, starting transfers between devices, shifted(): return lax.ppermute(value, axis, pairs)  80.4 us
    add x15, other arithmetic, turn(): passing[:, None, None] * later_now + local_grad  18.2 us
  transfers between devices with their start and end apart: 32, of which 31 were waited for; matrix products, arithmetic and copies ran while one was open for 2% of the time, Pallas kernels for 0%

commit v1 on v0

v1 whole, which is shorter than its diff:
```python
import math

import jax
import jax.numpy as jnp
from jax import lax
from jax.experimental import pallas as pl
from jax.experimental.pallas import tpu as pltpu
from jax.sharding import PartitionSpec as P

BLOCK = 128
HEAD_WIDTH = 64
STATE = 128
KERNEL = 4
ROWS = 8
EXTRA = 128
VMEM_BYTES = 50 * 1024 * 1024
F32 = jnp.float32
BF16 = jnp.bfloat16


def mm(left, right):
    return jnp.dot(left, right, preferred_element_type=F32)


def mm_nt(left, right):
    return lax.dot_general(left, right, (((1,), (1,)), ((), ())), preferred_element_type=F32)


def mm_tn(left, right):
    return lax.dot_general(left, right, (((0,), (0,)), ((), ())), preferred_element_type=F32)


def pieces_of(value, count):
    out = []
    for _ in range(count):
        piece = value.astype(BF16)
        out.append(piece)
        value = value - piece.astype(F32)
    return out


def exact_left(ones, value, count):
    return sum(mm(ones, piece) for piece in pieces_of(value, count))


def exact_right(value, ones, count):
    return sum(mm(piece, ones) for piece in pieces_of(value, count))


def spread_matrix(rows, columns):
    row = lax.broadcasted_iota(jnp.int32, (rows, columns), 0)
    lane = lax.broadcasted_iota(jnp.int32, (rows, columns), 1)
    return jnp.where((lane >> 6) == row, 1.0, 0.0).astype(BF16)


def gather_matrix(rows, columns):
    row = lax.broadcasted_iota(jnp.int32, (rows, columns), 0)
    lane = lax.broadcasted_iota(jnp.int32, (rows, columns), 1)
    return jnp.where((row >> 6) == lane, 1.0, 0.0).astype(BF16)


def softplus(value):
    small = jnp.exp(-jnp.abs(value))
    series = small * (1.0 - small * (0.5 - small * (1.0 / 3.0 - small * 0.25)))
    return jnp.maximum(value, 0.0) + jnp.where(small < 0.01, series, jnp.log(1.0 + small))


def block_marks(flags):
    row = lax.broadcasted_iota(jnp.int32, (BLOCK, BLOCK), 0)
    lane = lax.broadcasted_iota(jnp.int32, (BLOCK, BLOCK), 1)
    lower = jnp.where(row >= lane, 1.0, 0.0)
    upper = jnp.where(row <= lane, 1.0, 0.0)
    seg_col = jnp.sum(lower * flags, axis=1, keepdims=True)
    seg_row = mm(jnp.broadcast_to(flags, (8, BLOCK)).astype(BF16), upper.astype(BF16))[0:1]
    last = jnp.sum(flags, axis=1, keepdims=True)
    mask = jnp.where(seg_col == seg_row, lower, 0.0)
    alive = jnp.where(seg_col == 0.0, 1.0, 0.0)
    tail = jnp.where(seg_col == last, 1.0, 0.0)
    alive_last = jnp.where(last == 0.0, 1.0, 0.0)
    return mask, alive, tail, alive_last


def head_steps(raw, bias, power, length):
    rate = -0.5 * jnp.exp((power.astype(F32) / 3.0 - 1.0) * math.log(length))
    step = softplus(raw + bias)
    return step, rate


def block_scales(step, rate):
    row = lax.broadcasted_iota(jnp.int32, (BLOCK, BLOCK), 0)
    lane = lax.broadcasted_iota(jnp.int32, (BLOCK, BLOCK), 1)
    lower = jnp.where(row >= lane, 1.0, 0.0).astype(BF16)
    cum = exact_left(lower, step * rate, 3)
    total = cum[BLOCK - 1 : BLOCK]
    middle = 0.5 * total
    return jnp.exp(cum - middle), step * jnp.exp(middle - cum), jnp.exp(middle), jnp.exp(total)


def front_kernel(
    length, input_ref, rim_ref, raw_ref, flags_ref, power_ref, weight_ref, bias_ref, step_bias_ref, grad_ref,
    act_ref, slope_ref, bx_ref, ady_ref, pack_ref, padded,
):
    tokens, channels = input_ref.shape
    heads = raw_ref.shape[1]
    inner = heads * HEAD_WIDTH
    padded[0:8, :] = jnp.zeros((8, channels), F32)
    padded[8 - (KERNEL - 1) : 8, :] = rim_ref[...].astype(F32)
    padded[8 : 8 + tokens, :] = input_ref[...].astype(F32)
    weight = weight_ref[...].astype(F32)
    for low in range(0, channels, 128):
        cols = slice(low, low + 128)
        for start in range(0, tokens, 64):
            total = jnp.broadcast_to(bias_ref[:, cols], (64, 128))
            for tap in range(KERNEL):
                at = 8 - (KERNEL - 1) + start + tap
                total = total + padded[at : at + 64, cols] * weight[tap : tap + 1, cols]
            gate = 1.0 / (1.0 + jnp.exp(-total))
            act_ref[start : start + 64, cols] = (total * gate).astype(BF16)
            slope_ref[start : start + 64, cols] = gate * (1.0 + total * (1.0 - gate))

    step, rate = head_steps(raw_ref[...], step_bias_ref[...], power_ref[...], length)
    spread = spread_matrix(heads, inner)
    flags = flags_ref[...].astype(F32)
    blocks = tokens // BLOCK
    fresh, back, passing = [], [], []
    passing_heads = jnp.ones((1, heads), F32)
    for block in range(blocks):
        rows = slice(block * BLOCK, (block + 1) * BLOCK)
        _, alive, tail, alive_last = block_marks(flags[block : block + 1])
        row_scale, col_scale, half, whole = block_scales(step[rows], rate)
        through = whole * alive_last
        passing_heads = passing_heads * through
        line = lax.broadcasted_iota(jnp.int32, (8, heads), 0)
        both = exact_right(jnp.where(line == 0, half, through), spread, 3)
        half_wide, through_wide = both[0:1], both[1:2]
        bx = (act_ref[rows, 0:inner].astype(F32) * exact_right(col_scale, spread, 2)).astype(BF16)
        ady = (grad_ref[rows, :].astype(F32) * exact_right(row_scale, spread, 2)).astype(BF16)
        bx_ref[rows, :] = bx
        ady_ref[rows, :] = ady
        keys = (act_ref[rows, inner : inner + STATE].astype(F32) * tail).astype(BF16)
        queries = (act_ref[rows, inner + STATE : inner + 2 * STATE].astype(F32) * alive).astype(BF16)
        fresh.append(mm_tn(keys, bx) * half_wide)
        back.append(mm_tn(queries, ady) * half_wide)
        passing.append(through_wide)
    up = fresh[0]
    for block in range(1, blocks):
        up = passing[block] * up + fresh[block]
    down = back[blocks - 1]
    for block in range(blocks - 2, -1, -1):
        down = passing[block] * down + back[block]
    chunks = STATE // ROWS
    pack_ref[:, :, 0:inner] = jnp.concatenate(
        [up.reshape(chunks, ROWS, inner), down.reshape(chunks, ROWS, inner)], axis=1
    ).astype(BF16)
    hi, mid, lo = [piece.astype(F32) for piece in pieces_of(passing_heads, 3)]
    line = lax.broadcasted_iota(jnp.int32, (2 * ROWS, heads), 0)
    stack = jnp.where(line == 0, hi, jnp.where(line == 1, mid, jnp.where(line == 2, lo, 0.0)))
    row = lax.broadcasted_iota(jnp.int32, (heads, EXTRA), 0)
    lane = lax.broadcasted_iota(jnp.int32, (heads, EXTRA), 1)
    wide = mm(stack.astype(BF16), jnp.where(row == lane, 1.0, 0.0).astype(BF16))
    pack_ref[:, :, inner : inner + EXTRA] = jnp.broadcast_to(wide[None], (chunks, 2 * ROWS, EXTRA)).astype(BF16)


def scan_kernel(pack_ref, out_ref):
    devices, _, width = pack_ref.shape
    inner = width - EXTRA
    spread = spread_matrix(EXTRA, inner)
    passing = []
    for device in range(devices):
        passing.append(jnp.sum(mm(pack_ref[device, :, inner:width], spread), axis=0, keepdims=True))
    before, after = [None] * devices, [None] * devices
    up = jnp.zeros((ROWS, inner), F32)
    down = jnp.zeros((ROWS, inner), F32)
    for device in range(devices):
        before[device] = up
        up = passing[device] * up + pack_ref[device, :, 0:inner].astype(F32)[0:ROWS]
    for device in range(devices - 1, -1, -1):
        after[device] = down
        down = passing[device] * down + pack_ref[device, :, 0:inner].astype(F32)[ROWS : 2 * ROWS]
    for device in range(devices):
        out_ref[device] = jnp.concatenate([before[device], after[device]], axis=0).astype(BF16)


def back_kernel(
    length, carry_ref, act_ref, slope_ref, bx_ref, ady_ref, grad_ref, input_ref, rim_ref, raw_ref, flags_ref,
    power_ref, weight_ref, step_bias_ref, skip_ref,
    out_ref, edge_ref, head_ref, raw_out_ref, sums_ref, padded, dpre,
):
    tokens, channels = input_ref.shape
    heads = raw_ref.shape[1]
    inner = heads * HEAD_WIDTH
    blocks = tokens // BLOCK
    raw = raw_ref[...]
    step, rate = head_steps(raw, step_bias_ref[...], power_ref[...], length)
    spread = spread_matrix(heads, inner)
    gather = gather_matrix(inner, heads)
    flags = flags_ref[...].astype(F32)
    carry = carry_ref[...].astype(F32)
    entering = carry[:, 0:ROWS].reshape(STATE, inner)
    leaving = carry[:, ROWS : 2 * ROWS].reshape(STATE, inner)
    skip_wide = exact_right(jnp.broadcast_to(skip_ref[...], (8, heads)), spread, 3)[0:1]

    marks, scales, keys, queries, fresh, back, halves, throughs = [], [], [], [], [], [], [], []
    for block in range(blocks):
        rows = slice(block * BLOCK, (block + 1) * BLOCK)
        mark = block_marks(flags[block : block + 1])
        scale = block_scales(step[rows], rate)
        marks.append(mark)
        scales.append(scale)
        line = lax.broadcasted_iota(jnp.int32, (8, heads), 0)
        both = exact_right(jnp.where(line == 0, scale[2], scale[3] * mark[3]), spread, 3)
        halves.append(both[0:1])
        throughs.append(both[1:2])
        keys.append((act_ref[rows, inner : inner + STATE].astype(F32) * mark[2]).astype(BF16))
        queries.append((act_ref[rows, inner + STATE : inner + 2 * STATE].astype(F32) * mark[1]).astype(BF16))
        fresh.append(mm_tn(keys[block], bx_ref[rows, :]))
        back.append(mm_tn(queries[block], ady_ref[rows, :]))
    states = [entering]
    for block in range(blocks - 1):
        states.append(throughs[block] * states[block] + halves[block] * fresh[block])
    grads = [None] * blocks
    grads[blocks - 1] = leaving
    for block in range(blocks - 1, 0, -1):
        grads[block - 1] = throughs[block] * grads[block] + halves[block] * back[block]

    row = lax.broadcasted_iota(jnp.int32, (BLOCK, BLOCK), 0)
    lane = lax.broadcasted_iota(jnp.int32, (BLOCK, BLOCK), 1)
    upper = jnp.where(row <= lane, 1.0, 0.0).astype(BF16)
    at_last = jnp.where(lax.broadcasted_iota(jnp.int32, (BLOCK, heads), 0) == BLOCK - 1, 1.0, 0.0)
    for block in range(blocks):
        rows = slice(block * BLOCK, (block + 1) * BLOCK)
        mask, alive, tail, alive_last = marks[block]
        state = (halves[block] * states[block]).astype(BF16)
        grad = (halves[block] * grads[block]).astype(BF16)
        bx = bx_ref[rows, :]
        ady = ady_ref[rows, :]
        key = act_ref[rows, inner : inner + STATE]
        query = act_ref[rows, inner + STATE : inner + 2 * STATE]
        scores = mask * mm_nt(query, key)
        scores_t = scores.T.astype(BF16)
        scores = scores.astype(BF16)
        result = mm(scores, bx) + mm(queries[block], state)
        row_sum = exact_right(ady.astype(F32) * result, gather, 2)
        dbx = mm(scores_t, ady) + mm(keys[block], grad)
        col_sum = exact_right(bx.astype(F32) * dbx, gather, 2)
        dscores = mask * mm_nt(ady, bx)
        dscores_t = dscores.T.astype(BF16)
        dquery = mm(dscores.astype(BF16), key) + alive * mm_nt(ady, state)
        dkey = mm(dscores_t, query) + tail * mm_nt(bx, grad)
        whole = jnp.sum(
            grad.astype(F32) * fresh[block] + throughs[block] * (grads[block] * states[block]), axis=0, keepdims=True
        )
        whole = exact_right(jnp.broadcast_to(whole, (8, inner)), gather, 3)[0:1]
        dlog = exact_left(upper, row_sum - col_sum + at_last * whole, 3)
        dstep = col_sum / step[rows] + rate * dlog
        raw_out_ref[rows, :] = dstep / (1.0 + jnp.exp(-(raw[rows] + step_bias_ref[...])))
        dx = exact_right(scales[block][1], spread, 2) * dbx + skip_wide * grad_ref[rows, :].astype(F32)
        dpre[rows, 0:inner] = dx * slope_ref[rows, 0:inner]
        dpre[rows, inner : inner + STATE] = dkey * slope_ref[rows, inner : inner + STATE]
        dpre[rows, inner + STATE : channels] = dquery * slope_ref[rows, inner + STATE : channels]

    dpre[tokens : tokens + 8, :] = jnp.zeros((8, channels), F32)
    padded[0:8, :] = jnp.zeros((8, channels), F32)
    padded[8 - (KERNEL - 1) : 8, :] = rim_ref[...].astype(F32)
    padded[8 : 8 + tokens, :] = input_ref[...].astype(F32)
    weight = weight_ref[...].astype(F32)
    for low in range(0, channels, 128):
        cols = slice(low, low + 128)
        acc = [jnp.zeros((8, 128), F32) for _ in range(KERNEL + 1)]
        for start in range(0, tokens, 64):
            here = dpre[start : start + 64, cols]
            total = here * weight[KERNEL - 1 : KERNEL, cols]
            for tap in range(KERNEL - 1):
                ahead = start + KERNEL - 1 - tap
                total = total + dpre[ahead : ahead + 64, cols] * weight[tap : tap + 1, cols]
            out_ref[start : start + 64, cols] = total.astype(BF16)
            if start == tokens - 64:
                edge_ref[:, cols] = total[48:64]
            for tap in range(KERNEL):
                at = 8 - (KERNEL - 1) + start + tap
                acc[tap] = acc[tap] + jnp.sum((here * padded[at : at + 64, cols]).reshape(8, 8, 128), axis=0)
            acc[KERNEL] = acc[KERNEL] + jnp.sum(here.reshape(8, 8, 128), axis=0)
        line = lax.broadcasted_iota(jnp.int32, (8, 128), 0)
        block_sums = jnp.zeros((8, 128), F32)
        for tap in range(KERNEL + 1):
            block_sums = jnp.where(line == tap, jnp.sum(acc[tap], axis=0, keepdims=True), block_sums)
        sums_ref[:, cols] = block_sums
        first = [dpre[at : at + 1, cols] for at in range(KERNEL - 1)]
        lines = jnp.zeros((8, 128), F32)
        for at in range(KERNEL - 1):
            part = sum(weight[tap : tap + 1, cols] * first[at - tap] for tap in range(at + 1))
            lines = jnp.where(line == at, part, lines)
        head_ref[:, cols] = lines


def call(kernel, out_shape, scratch=(), flops=0, moved=0):
    return pl.pallas_call(
        kernel,
        out_shape=out_shape,
        scratch_shapes=list(scratch),
        compiler_params=pltpu.CompilerParams(vmem_limit_bytes=VMEM_BYTES),
        cost_estimate=pl.CostEstimate(flops=flops, bytes_accessed=moved, transcendentals=0),
    )


def shifted(value, axis, by):
    devices = lax.axis_size(axis)
    pairs = [(i, i + by) for i in range(devices) if 0 <= i + by < devices]
    return lax.ppermute(value, axis, pairs)


def body(
    conv_input, step_raw, doc_starts, decay_power, conv_weight, conv_bias, step_bias, skip_gain, grad_out
):
    tokens, channels = conv_input.shape[1:]
    heads = step_raw.shape[2]
    inner = heads * HEAD_WIDTH
    ctx_size = lax.axis_size("ctx")
    dp_size = lax.axis_size("dp")
    length = tokens * ctx_size
    chunks = STATE // ROWS
    inputs = conv_input[0]
    rim = shifted(inputs[tokens - (KERNEL - 1) :], "ctx", 1)
    raw = step_raw[0]
    flags = doc_starts.reshape(tokens // BLOCK, BLOCK)
    power = decay_power[None]
    step_bias = step_bias[None]
    skip = skip_gain[None]
    grads = grad_out[0]
    shape = jax.ShapeDtypeStruct

    act, slope, bx, ady, pack = call(
        lambda *refs: front_kernel(length, *refs),
        (
            shape((tokens, channels), BF16),
            shape((tokens, channels), F32),
            shape((tokens, inner), BF16),
            shape((tokens, inner), BF16),
            shape((chunks, 2 * ROWS, inner + EXTRA), BF16),
        ),
        [pltpu.VMEM((tokens + 8, channels), F32)],
    )(inputs, rim, raw, flags, power, conv_weight, conv_bias[None], step_bias, grads)

    gathered = lax.all_to_all(pack, "ctx", 0, 0, tiled=True)
    scanned = call(scan_kernel, shape((ctx_size, 2 * ROWS, inner), BF16))(gathered)
    carry = lax.all_to_all(scanned, "ctx", 0, 0, tiled=True)

    out, edge, head, grad_raw, sums = call(
        lambda *refs: back_kernel(length, *refs),
        (
            shape((tokens, channels), BF16),
            shape((16, channels), F32),
            shape((8, channels), F32),
            shape((tokens, heads), F32),
            shape((8, channels), F32),
        ),
        [pltpu.VMEM((tokens + 8, channels), F32), pltpu.VMEM((tokens + 8, channels), F32)],
    )(carry, act, slope, bx, ady, grads, inputs, rim, raw, flags, power, conv_weight, step_bias, skip)

    devices = dp_size * ctx_size
    width = channels // devices
    terms = sums[: KERNEL + 1].reshape(KERNEL + 1, devices, width).transpose(1, 0, 2)
    shard = jnp.sum(lax.all_to_all(terms, ("dp", "ctx"), 0, 0, tiled=True), axis=0)
    shard = shard * (1.0 / (dp_size * length))
    back = shifted(head[: KERNEL - 1], "ctx", -1)
    edge = jnp.concatenate([edge[: 16 - (KERNEL - 1)], edge[16 - (KERNEL - 1) :] + back], 0)
    grad_input = lax.dynamic_update_slice(out, edge.astype(BF16), (tokens - 16, 0))
    return (grad_input[None], grad_raw[None], shard[:KERNEL][:, None, :], shard[KERNEL][None, :])


def solution(mesh):
    return jax.shard_map(
        body,
        mesh=mesh,
        in_specs=(
            P("dp", "ctx", "tp"),
            P("dp", "ctx", "tp"),
            P("dp", "ctx"),
            P("tp"),
            P(None, "tp"),
            P("tp"),
            P("tp"),
            P("tp"),
            P("dp", "ctx", "tp"),
        ),
        out_specs=(
            P("dp", "ctx", "tp"),
            P("dp", "ctx", "tp"),
            P(None, "tp", ("dp", "ctx")),
            P("tp", ("dp", "ctx")),
        ),
        check_vma=False,
    )
```

time: 706 us -> 144 us (0.20)
  blocking collectives: 276 us -> 82.1 us
  waiting for transfers between devices: 185 us -> 19.5 us
  other arithmetic: 76.8 us -> 0.73 us
  starting transfers between devices: 80.4 us -> 18.1 us
  local copies, waits for them, and re-layouts: 57.9 us -> 9.86 us
  matrix products: 21.7 us -> 0 us
  Pallas kernels: 0 us -> 12.2 us
    unnamed x1 -> x0, blocking collectives: 276 us -> none
    ppermute x32 -> x2, waiting for transfers between devices: 185 us -> 0.01 us  [shifted(): return lax.ppermute(value, axis, pairs)]
    all_to_all x0 -> x2, blocking collectives: none -> 82.1 us  [the longest x1 50.3 us: body(): gathered = lax.all_to_all(pack, 'ctx', 0, 0, tiled=True)]
    ppermute x32 -> x2, starting transfers between devices: 80.4 us -> 5.09 us  [shifted(): return lax.ppermute(value, axis, pairs)]
    dot_general x25 -> x0, matrix products: 21.7 us -> none  [the longest x4 8.21 us: block_step(): jnp.einsum('hts,shp->thp', mixing, values, preferred_element_type=jnp.flo...]
    all_to_all x0 -> x1, waiting for transfers between devices: none -> 19.5 us  [body(): lax.all_to_all(terms, ('dp', 'ctx'), 0, 0, tiled=True)]
    add x15 -> x0, other arithmetic: 18.2 us -> none  [turn(): passing[:, None, None] * later_now + local_grad]
    dynamic_update_slice x40 -> x0, local copies, waits for them, and re-layouts: 13.6 us -> none  [run_blocks(): lax.scan(lambda carry, item: block_step(carry, item, skip_gain), state, p...]
  transfers between devices with their start and end apart: 32 -> 3, of which waited for: 31 -> 1; matrix products, arithmetic and copies ran while one was open for 2% -> 3% of each run, Pallas kernels for 0% -> 0%
where the time goes in v1:
time: 144 us; the launch traced here: 143 us
  blocking collectives  82.1 us (57%)
  waiting for transfers between devices  19.5 us (14%)
  starting transfers between devices  18.1 us (13%)
  Pallas kernels  12.2 us (8%)
  local copies, waits for them, and re-layouts  9.86 us (7%)
    all_to_all x1, blocking collectives, body(): gathered = lax.all_to_all(pack, 'ctx', 0, 0, tiled=True)  50.3 us
    all_to_all x1, blocking collectives, body(): carry = lax.all_to_all(scanned, 'ctx', 0, 0, tiled=True)  31.7 us
    all_to_all x1, waiting for transfers between devices, body(): lax.all_to_all(terms, ('dp', 'ctx'), 0, 0, tiled=True)  19.5 us
    all_to_all x1, starting transfers between devices, body(): lax.all_to_all(terms, ('dp', 'ctx'), 0, 0, tiled=True)  13 us
    pallas_call x1, Pallas kernels, body(): call(lambda *refs: back_kernel(length, *refs), (shape((tokens, channels),...  7.45 us
    unnamed x28, local copies, waits for them, and re-layouts  6.34 us
    ppermute x2, starting transfers between devices, shifted(): return lax.ppermute(value, axis, pairs)  5.09 us
    pallas_call x1, Pallas kernels, body(): call(lambda *refs: front_kernel(length, *refs), (shape((tokens, channels)...  4 us
  transfers between devices with their start and end apart: 3, of which 1 were waited for; matrix products, arithmetic and copies ran while one was open for 3% of the time, Pallas kernels for 0%

profile of v1, /device:TPU:24, one launch (start us, length us, event | category | flops | bytes accessed | tf_op | source)
XLA Modules:
  0.0 143.3 jit_solution(10054616771437782788)
XLA Ops:
  0.6 0.7 slice_bitcast_fusion
  1.4 3.8 %collective-permute-start = (bf16[3,1280]{1,0:T(4,128)(2,1)S(1)}, bf16[3,1280]{1,0:T(4,128)(2,1)S(1)}, u32[]{:S(2)}, u32[]{:S(2)}) collective-permute-start(bf16[3,1280]{1,0:T(4,128)(2,1)S(1)} %slice_bitcast_fusion), channel_id=1, source_target_pairs={{0,8},{8,16},{16,24},{24,32},{32,40},{40,48},{48,56},{56,64},{64,7... | collective-permute-start | bytes 23048 | tf_op jit(solution)/shard_map/ppermute | solution.py:309
  5.2 0.7 broadcast_in_dim.22.refs_6_
  5.9 0.8 copy.19
  6.7 0.0 collective-permute-done.refs_1_.refs_7_
  6.7 0.0 copy-start
  6.7 1.1 copy-done
  7.8 1.0 copy-done.2
  8.8 0.7 copy-done.4
  9.6 0.7 copy-done.6
  10.2 0.7 copy-done.8
  10.9 0.7 copy-done.10
  11.5 4.0 %shard_map.120 = (bf16[256,1280]{1,0:T(8,128)(2,1)S(1)}, f32[256,1280]{1,0:T(8,128)}, bf16[256,1024]{1,0:T(8,128)(2,1)S(1)}, bf16[256,1024]{1,0:T(8,128)(2,1)S(1)}, bf16[16,16,1152]{2,1,0:T(8,128)(2,1)S(1)}) custom-call(bf16[256,1280]{1,0:T(8,128)(2,1)S(1)} %bitcast.20, bf16[3,1280]{1,0:T(4,128)(2,1)S(1)} %collective-permute-done.refs_1_.refs_7_, ...), custom_call_target="tpu_custom_call" | custom-call | tf_op jit(solution)/shard_map/pallas_call | solution.py:332
  15.5 50.3 %all_to_all.15.pack_ref = bf16[16,16,1152]{2,1,0:T(8,128)(2,1)S(1)} all-to-all(bf16[16,16,1152]{2,1,0:T(8,128)(2,1)S(1)} %get-tuple-element.14), channel_id=1, replica_groups=mesh['dp'=4,'ctx'=16,'tp'=8] {'ctx'}, dimensions={0} | all-to-all | bytes 1179648 | tf_op jit(solution)/shard_map/all_to_all | solution.py:344
  65.9 0.0 copy-start.9
  65.9 0.0 copy-start.11
  65.9 0.0 copy-start.12
  65.9 0.7 shard_map.121
  66.7 31.7 %all_to_all.16.refs_0_ = bf16[16,16,1024]{2,1,0:T(8,128)(2,1)S(1)} all-to-all(bf16[16,16,1024]{2,1,0:T(8,128)(2,1)S(1)} %shard_map.121), channel_id=1, replica_groups=mesh['dp'=4,'ctx'=16,'tp'=8] {'ctx'}, dimensions={0} | all-to-all | bytes 1048576 | tf_op jit(solution)/shard_map/all_to_all | solution.py:346
  98.4 0.0 copy-done.3
  98.5 7.4 %shard_map.122 = (bf16[256,1280]{1,0:T(8,128)(2,1)}, f32[16,1280]{1,0:T(8,128)S(1)}, f32[8,1280]{1,0:T(8,128)S(1)}, f32[256,16]{1,0:T(8,128)S(1)}, f32[8,1280]{1,0:T(8,128)S(1)}) custom-call(bf16[16,16,1024]{2,1,0:T(8,128)(2,1)S(1)} %all_to_all.16.refs_0_, bf16[256,1280]{1,0:T(8,128)(2,1)S(1)} %get-tuple-element.15.refs_1_, ...), custom_call_target="tpu_custom_call" | custom-call | tf_op jit(solution)/shard_map/pallas_call | solution.py:348
  105.9 1.3 collective-permute-start.1
  107.2 0.7 copy.21
  107.9 0.2 reshape.49
  108.1 0.8 copy.20
  108.9 13.0 %all-to-all-start.2 = ((f32[64,5,20]{2,1,0:T(8,128)}), f32[64,5,20]{2,1,0:T(8,128)S(1)}, u32[]{:S(2)}, u32[]{:S(2)}) async-start(f32[64,5,20]{2,1,0:T(8,128)} %copy.20), calls=%async_computation.2 | async-start | bytes 524288 | tf_op jit(solution)/shard_map/all_to_all | solution.py:363
  121.9 0.0 collective-permute-done.1
  121.9 0.6 maximum_dynamic-update-slice_fusion
  122.6 19.5 %all-to-all-done.2 = f32[64,5,20]{2,1,0:T(8,128)S(1)} async-done(((f32[64,5,20]{2,1,0:T(8,128)}), f32[64,5,20]{2,1,0:T(8,128)S(1)}, u32[]{:S(2)}, u32[]{:S(2)}) %all-to-all-start.2) | async-done | bytes 25632 | tf_op jit(solution)/shard_map/all_to_all | solution.py:363
  142.1 0.1 reduce_sum.9
  142.2 0.5 slice.32
  142.7 0.6 slice.31
  (19 shorter events, 0.1 us)
Async XLA Ops:
  1.4 5.3 %collective-permute-start = (bf16[3,1280]{1,0:T(4,128)(2,1)S(1)}, bf16[3,1280]{1,0:T(4,128)(2,1)S(1)}, u32[]{:S(2)}, u32[]{:S(2)}) collective-permute-start(bf16[3,1280]{1,0:T(4,128)(2,1)S(1)} %slice_bitcast_fusion), channel_id=1, source_target_pairs={{0,8},{8,16},{16,24},{24,32},{32,40},{40,48},{48,56},{56,64},{64,7... | collective-permute-start | bytes 23048 | tf_op jit(solution)/shard_map/ppermute | solution.py:309
  6.7 1.1 copy-start
  7.8 1.0 copy-start.2
  8.8 0.7 copy-start.4
  9.5 0.7 copy-start.6
  10.2 0.7 copy-start.8
  10.9 0.7 copy-start.10
  65.9 32.5 %copy-start.1 = (bf16[1,256,1280]{2,1,0:T(8,128)(2,1)S(1)}, bf16[1,256,1280]{2,1,0:T(8,128)(2,1)}, u32[]{:S(2)}) copy-start(bf16[1,256,1280]{2,1,0:T(8,128)(2,1)} %param.9) | copy-start | bytes 1966084
  65.9 32.5 %copy-start.3 = (bf16[1,256,1024]{2,1,0:T(8,128)(2,1)S(1)}, bf16[1,256,1024]{2,1,0:T(8,128)(2,1)}, u32[]{:S(2)}) copy-start(bf16[1,256,1024]{2,1,0:T(8,128)(2,1)} %param.17) | copy-start | bytes 1572868
  65.9 32.5 %copy-start.5 = (bf16[4,1280]{1,0:T(4,128)(2,1)S(1)}, bf16[4,1280]{1,0:T(4,128)(2,1)}, u32[]{:S(2)}) copy-start(bf16[4,1280]{1,0:T(4,128)(2,1)} %refs_11_.1) | copy-start | bytes 30724
  65.9 32.5 %copy-start.7 = (s32[1,256]{1,0:T(1,128)S(1)}, s32[1,256]{1,0:T(1,128)}, u32[]{:S(2)}) copy-start(s32[1,256]{1,0:T(1,128)} %param.11) | copy-start | bytes 3076
  65.9 32.5 %copy-start.9 = (s32[16]{0:T(128)S(1)}, s32[16]{0:T(128)}, u32[]{:S(2)}) copy-start(s32[16]{0:T(128)} %param.12) | copy-start | bytes 196
  65.9 32.5 %copy-start.11 = (f32[16]{0:T(128)S(1)}, f32[16]{0:T(128)}, u32[]{:S(2)}) copy-start(f32[16]{0:T(128)} %param.15) | copy-start | bytes 196
  65.9 32.5 %copy-start.12 = (f32[16]{0:T(128)S(1)}, f32[16]{0:T(128)}, u32[]{:S(2)}) copy-start(f32[16]{0:T(128)} %param.16) | copy-start | bytes 196
  105.9 16.0 %collective-permute-start.1 = (f32[3,1280]{1,0:T(4,128)S(1)}, f32[3,1280]{1,0:T(4,128)S(1)}, u32[]{:S(2)}, u32[]{:S(2)}) collective-permute-start(f32[3,1280]{1,0:T(4,128)S(1)} %slice.29), channel_id=1, source_target_pairs={{8,0},{16,8},{24,16},{32,24},{40,32},{48,40},{56,48},{64,56},{72,6... | collective-permute-start | bytes 46088 | tf_op jit(solution)/shard_map/ppermute | solution.py:309
  108.9 33.2 %all-to-all-start.2 = ((f32[64,5,20]{2,1,0:T(8,128)}), f32[64,5,20]{2,1,0:T(8,128)S(1)}, u32[]{:S(2)}, u32[]{:S(2)}) async-start(f32[64,5,20]{2,1,0:T(8,128)} %copy.20), calls=%async_computation.2 | async-start | bytes 524288 | tf_op jit(solution)/shard_map/all_to_all | solution.py:363

commit v2 on v1

--- a/solution.py
+++ b/solution.py
@@ -11,11 +11,13 @@
 HEAD_WIDTH = 64
 STATE = 128
 KERNEL = 4
-ROWS = 8
+SPLIT = 4
+ROWS = STATE // SPLIT
 EXTRA = 128
 VMEM_BYTES = 50 * 1024 * 1024
 F32 = jnp.float32
 BF16 = jnp.bfloat16
+CTX = ("ch", "cl")
 
 
 def mm(left, right):
@@ -148,43 +150,78 @@
     down = back[blocks - 1]
     for block in range(blocks - 2, -1, -1):
         down = passing[block] * down + back[block]
-    chunks = STATE // ROWS
     pack_ref[:, :, 0:inner] = jnp.concatenate(
-        [up.reshape(chunks, ROWS, inner), down.reshape(chunks, ROWS, inner)], axis=1
+        [up.reshape(SPLIT, ROWS, inner), down.reshape(SPLIT, ROWS, inner)], axis=1
     ).astype(BF16)
-    hi, mid, lo = [piece.astype(F32) for piece in pieces_of(passing_heads, 3)]
-    line = lax.broadcasted_iota(jnp.int32, (2 * ROWS, heads), 0)
-    stack = jnp.where(line == 0, hi, jnp.where(line == 1, mid, jnp.where(line == 2, lo, 0.0)))
     row = lax.broadcasted_iota(jnp.int32, (heads, EXTRA), 0)
     lane = lax.broadcasted_iota(jnp.int32, (heads, EXTRA), 1)
-    wide = mm(stack.astype(BF16), jnp.where(row == lane, 1.0, 0.0).astype(BF16))
-    pack_ref[:, :, inner : inner + EXTRA] = jnp.broadcast_to(wide[None], (chunks, 2 * ROWS, EXTRA)).astype(BF16)
-
-
-def scan_kernel(pack_ref, out_ref):
-    devices, _, width = pack_ref.shape
-    inner = width - EXTRA
+    place = jnp.where(row == lane, 1.0, 0.0).astype(BF16)
+    wide = exact_right(jnp.broadcast_to(passing_heads, (8, heads)), place, 3)[0:1]
+    pack_ref[:, :, inner : inner + EXTRA] = jnp.broadcast_to(
+        stacked(wide, 2 * ROWS)[None], (SPLIT, 2 * ROWS, EXTRA)
+    )
+
+
+def stacked(value, rows):
+    hi, mid, lo = [piece.astype(F32) for piece in pieces_of(value, 3)]
+    line = lax.broadcasted_iota(jnp.int32, (rows, EXTRA), 0)
+    return jnp.where(line == 0, hi, jnp.where(line == 1, mid, jnp.where(line == 2, lo, 0.0))).astype(BF16)
+
+
+def passed(pack_ref, source, inner, spread):
+    lines = pack_ref[source, 0:16, inner : inner + EXTRA]
+    return (
+        jnp.sum(lines.astype(F32), axis=0, keepdims=True),
+        jnp.sum(mm(lines, spread), axis=0, keepdims=True),
+    )
+
+
+def totals_kernel(near_ref, out_ref):
+    inner = near_ref.shape[2] - EXTRA
+    group = lax.axis_index("ch")
     spread = spread_matrix(EXTRA, inner)
-    passing = []
-    for device in range(devices):
-        passing.append(jnp.sum(mm(pack_ref[device, :, inner:width], spread), axis=0, keepdims=True))
-    before, after = [None] * devices, [None] * devices
+    decay = [passed(near_ref, source, inner, spread) for source in range(SPLIT)]
     up = jnp.zeros((ROWS, inner), F32)
     down = jnp.zeros((ROWS, inner), F32)
-    for device in range(devices):
-        before[device] = up
-        up = passing[device] * up + pack_ref[device, :, 0:inner].astype(F32)[0:ROWS]
-    for device in range(devices - 1, -1, -1):
-        after[device] = down
-        down = passing[device] * down + pack_ref[device, :, 0:inner].astype(F32)[ROWS : 2 * ROWS]
-    for device in range(devices):
-        out_ref[device] = jnp.concatenate([before[device], after[device]], axis=0).astype(BF16)
+    through = jnp.ones((1, EXTRA), F32)
+    for source in range(SPLIT):
+        up = decay[source][1] * up + near_ref[source, 0:ROWS, 0:inner].astype(F32)
+        through = through * decay[source][0]
+    for source in range(SPLIT - 1, -1, -1):
+        down = decay[source][1] * down + near_ref[source, ROWS : 2 * ROWS, 0:inner].astype(F32)
+    lines = stacked(through, ROWS)
+    for target in range(SPLIT):
+        later = jnp.where(target > group, 1.0, 0.0)
+        out_ref[target, :, 0:inner] = (later * up + (1.0 - later) * down).astype(BF16)
+        out_ref[target, :, inner : inner + EXTRA] = lines
+
+
+def states_kernel(near_ref, far_ref, out_ref):
+    inner = near_ref.shape[2] - EXTRA
+    group = lax.axis_index("ch")
+    spread = spread_matrix(EXTRA, inner)
+    near = [passed(near_ref, source, inner, spread)[1] for source in range(SPLIT)]
+    far = [passed(far_ref, source, inner, spread)[1] for source in range(SPLIT)]
+    up = jnp.zeros((ROWS, inner), F32)
+    down = jnp.zeros((ROWS, inner), F32)
+    for source in range(SPLIT):
+        use = jnp.where(source < group, 1.0, 0.0)
+        up = (use * far[source] + (1.0 - use)) * up + use * far_ref[source, :, 0:inner].astype(F32)
+    for source in range(SPLIT - 1, -1, -1):
+        use = jnp.where(source > group, 1.0, 0.0)
+        down = (use * far[source] + (1.0 - use)) * down + use * far_ref[source, :, 0:inner].astype(F32)
+    for source in range(SPLIT):
+        out_ref[source, 0:ROWS, :] = up.astype(BF16)
+        up = near[source] * up + near_ref[source, 0:ROWS, 0:inner].astype(F32)
+    for source in range(SPLIT - 1, -1, -1):
+        out_ref[source, ROWS : 2 * ROWS, :] = down.astype(BF16)
+        down = near[source] * down + near_ref[source, ROWS : 2 * ROWS, 0:inner].astype(F32)
 
 
 def back_kernel(
     length, carry_ref, act_ref, slope_ref, bx_ref, ady_ref, grad_ref, input_ref, rim_ref, raw_ref, flags_ref,
     power_ref, weight_ref, step_bias_ref, skip_ref,
-    out_ref, edge_ref, head_ref, raw_out_ref, sums_ref, padded, dpre,
+    out_ref, edge_ref, head_ref, raw_out_ref, terms_ref, padded, dpre, sums_ref,
 ):
     tokens, channels = input_ref.shape
     heads = raw_ref.shape[1]
@@ -292,6 +329,23 @@
             lines = jnp.where(line == at, part, lines)
         head_ref[:, cols] = lines
 
+    targets = terms_ref.shape[0]
+    width = channels // targets
+    line = lax.broadcasted_iota(jnp.int32, (8, 128), 0)
+    lane = lax.broadcasted_iota(jnp.int32, (8, 128), 1)
+    own = (lane >= line * width) & (lane < (line + 1) * width) & (line <= KERNEL)
+    for tile in range(channels // 128, sums_ref.shape[1] // 128):
+        sums_ref[:, tile * 128 : tile * 128 + 128] = jnp.zeros((8, 128), F32)
+    aside = pltpu.roll(sums_ref[...], 0, 1, stride=width // 2, stride_axis=0)
+    sums_ref[...] = pltpu.roll(aside, 0, 1, stride=width - width // 2, stride_axis=0)
+    for target in range(targets):
+        tile, at = divmod(target * width, 128)
+        part = sums_ref[:, tile * 128 : tile * 128 + 128]
+        if at:
+            part = jnp.where(lane >= at, part, sums_ref[:, tile * 128 + 128 : tile * 128 + 256])
+            part = pltpu.roll(part, 128 - at, 1)
+        terms_ref[target : target + 1, :] = jnp.sum(jnp.where(own, part, 0.0), axis=0, keepdims=True)
+
 
 def call(kernel, out_shape, scratch=(), flops=0, moved=0):
     return pl.pallas_call(
@@ -315,12 +369,12 @@
     tokens, channels = conv_input.shape[1:]
     heads = step_raw.shape[2]
     inner = heads * HEAD_WIDTH
-    ctx_size = lax.axis_size("ctx")
+    ctx_size = lax.axis_size(CTX)
     dp_size = lax.axis_size("dp")
+    devices = dp_size * ctx_size
     length = tokens * ctx_size
-    chunks = STATE // ROWS
     inputs = conv_input[0]
-    rim = shifted(inputs[tokens - (KERNEL - 1) :], "ctx", 1)
+    rim = shifted(inputs[tokens - (KERNEL - 1) :], CTX, 1)
     raw = step_raw[0]
     flags = doc_starts.reshape(tokens // BLOCK, BLOCK)
     power = decay_power[None]
@@ -336,58 +390,66 @@
             shape((tokens, channels), F32),
             shape((tokens, inner), BF16),
             shape((tokens, inner), BF16),
-            shape((chunks, 2 * ROWS, inner + EXTRA), BF16),
+            shape((SPLIT, 2 * ROWS, inner + EXTRA), BF16),
         ),
         [pltpu.VMEM((tokens + 8, channels), F32)],
     )(inputs, rim, raw, flags, power, conv_weight, conv_bias[None], step_bias, grads)
 
-    gathered = lax.all_to_all(pack, "ctx", 0, 0, tiled=True)
-    scanned = call(scan_kernel, shape((ctx_size, 2 * ROWS, inner), BF16))(gathered)
-    carry = lax.all_to_all(scanned, "ctx", 0, 0, tiled=True)
-
-    out, edge, head, grad_raw, sums = call(
+    near = lax.all_to_all(pack, "cl", 0, 0, tiled=True)
+    totals = call(totals_kernel, shape((SPLIT, ROWS, inner + EXTRA), BF16))(near)
+    far = lax.all_to_all(totals, "ch", 0, 0, tiled=True)
+    states = call(states_kernel, shape((SPLIT, 2 * ROWS, inner), BF16))(near, far)
+    carry = lax.all_to_all(states, "cl", 0, 0, tiled=True)
+
+    out, edge, head, grad_raw, terms = call(
         lambda *refs: back_kernel(length, *refs),
         (
             shape((tokens, channels), BF16),
             shape((16, channels), F32),
             shape((8, channels), F32),
             shape((tokens, heads), F32),
-            shape((8, channels), F32),
+            shape((devices, 128), F32),
         ),
-        [pltpu.VMEM((tokens + 8, channels), F32), pltpu.VMEM((tokens + 8, channels), F32)],
+        [
+            pltpu.VMEM((tokens + 8, channels), F32),
+            pltpu.VMEM((tokens + 8, channels), F32),
+            pltpu.VMEM((8, channels + 2 * 128), F32),
+        ],
     )(carry, act, slope, bx, ady, grads, inputs, rim, raw, flags, power, conv_weight, step_bias, skip)
 
-    devices = dp_size * ctx_size
+    terms = lax.all_to_all(terms, ("dp",) + CTX, 0, 0, tiled=True)
     width = channels // devices
-    terms = sums[: KERNEL + 1].reshape(KERNEL + 1, devices, width).transpose(1, 0, 2)
-    shard = jnp.sum(lax.all_to_all(terms, ("dp", "ctx"), 0, 0, tiled=True), axis=0)
+    shard = jnp.sum(terms, axis=0)[: (KERNEL + 1) * width].reshape(KERNEL + 1, width)
     shard = shard * (1.0 / (dp_size * length))
-    back = shifted(head[: KERNEL - 1], "ctx", -1)
+    back = shifted(head[: KERNEL - 1], CTX, -1)
     edge = jnp.concatenate([edge[: 16 - (KERNEL - 1)], edge[16 - (KERNEL - 1) :] + back], 0)
     grad_input = lax.dynamic_update_slice(out, edge.astype(BF16), (tokens - 16, 0))
     return (grad_input[None], grad_raw[None], shard[:KERNEL][:, None, :], shard[KERNEL][None, :])
 
 
 def solution(mesh):
+    sizes = mesh.shape
+    shape = (sizes["dp"], sizes["ctx"] // SPLIT, SPLIT, sizes["tp"])
+    mesh = jax.sharding.Mesh(mesh.devices.reshape(shape), ("dp",) + CTX + ("tp",))
     return jax.shard_map(
         body,
         mesh=mesh,
         in_specs=(
-            P("dp", "ctx", "tp"),
-            P("dp", "ctx", "tp"),
-            P("dp", "ctx"),
+            P("dp", CTX, "tp"),
+            P("dp", CTX, "tp"),
+            P("dp", CTX),
             P("tp"),
             P(None, "tp"),
             P("tp"),
             P("tp"),
             P("tp"),
-            P("dp", "ctx", "tp"),
+            P("dp", CTX, "tp"),
         ),
         out_specs=(
-            P("dp", "ctx", "tp"),
-            P("dp", "ctx", "tp"),
-            P(None, "tp", ("dp", "ctx")),
-            P("tp", ("dp", "ctx")),
+            P("dp", CTX, "tp"),
+            P("dp", CTX, "tp"),
+            P(None, "tp", ("dp",) + CTX),
+            P("tp", ("dp",) + CTX),
         ),
         check_vma=False,
     )

time: 144 us -> 118 us (0.82)
  blocking collectives: 82.1 us -> 68.1 us
  waiting for transfers between devices: 19.5 us -> 11.6 us
  starting transfers between devices: 18.1 us -> 15.3 us
    all_to_all x2 -> x3, blocking collectives: 82.1 us -> 68.1 us  [the longest x1 31.5 us: body(): far = lax.all_to_all(totals, 'ch', 0, 0, tiled=True)]
    all_to_all x1, waiting for transfers between devices: 19.5 us -> 7.94 us  [body(): terms = lax.all_to_all(terms, ('dp',) + CTX, 0, 0, tiled=True)]
    ppermute x2, waiting for transfers between devices: 0.01 us -> 3.69 us  [shifted(): return lax.ppermute(value, axis, pairs)]
    all_to_all x1, starting transfers between devices: 13 us -> 10.2 us  [body(): terms = lax.all_to_all(terms, ('dp',) + CTX, 0, 0, tiled=True)]
  transfers between devices with their start and end apart: 3 -> 3, of which waited for: 1 -> 2; matrix products, arithmetic and copies ran while one was open for 3% -> 2% of each run, Pallas kernels for 0% -> 0%
where the time goes in v2:
time: 118 us
  blocking collectives  68.1 us (58%)
  starting transfers between devices  15.3 us (13%)
  Pallas kernels  12 us (10%)
  waiting for transfers between devices  11.6 us (10%)
  local copies, waits for them, and re-layouts  9.04 us (8%)
    all_to_all x1, blocking collectives, body(): far = lax.all_to_all(totals, 'ch', 0, 0, tiled=True)  31.5 us
    all_to_all x1, blocking collectives, body(): near = lax.all_to_all(pack, 'cl', 0, 0, tiled=True)  22.5 us
    all_to_all x1, blocking collectives, body(): carry = lax.all_to_all(states, 'cl', 0, 0, tiled=True)  14.1 us
    all_to_all x1, starting transfers between devices, body(): terms = lax.all_to_all(terms, ('dp',) + CTX, 0, 0, tiled=True)  10.2 us
    all_to_all x1, waiting for transfers between devices, body(): terms = lax.all_to_all(terms, ('dp',) + CTX, 0, 0, tiled=True)  7.94 us
    pallas_call x1, Pallas kernels, body(): call(lambda *refs: back_kernel(length, *refs), (shape((tokens, channels),...  7.12 us
    unnamed x28, local copies, waits for them, and re-layouts  6.34 us
    ppermute x2, starting transfers between devices, shifted(): return lax.ppermute(value, axis, pairs)  5.1 us
  transfers between devices with their start and end apart: 3, of which 2 were waited for; matrix products, arithmetic and copies ran while one was open for 2% of the time, Pallas kernels for 0%

profile of v2, /device:TPU:24, one launch (start us, length us, event | category | flops | bytes accessed | tf_op | source)
XLA Modules:
  0.0 117.6 jit_solution(11430800579926583684)
XLA Ops:
  0.6 0.7 slice_bitcast_fusion
  1.4 3.8 %collective-permute-start = (bf16[3,1280]{1,0:T(4,128)(2,1)S(1)}, bf16[3,1280]{1,0:T(4,128)(2,1)S(1)}, u32[]{:S(2)}, u32[]{:S(2)}) collective-permute-start(bf16[3,1280]{1,0:T(4,128)(2,1)S(1)} %slice_bitcast_fusion), channel_id=1, source_target_pairs={{0,8},{8,16},{16,24},{24,32},{32,40},{40,48},{48,56},{56,64},{64,7... | collective-permute-start | bytes 23048 | tf_op jit(solution)/shard_map/ppermute | solution.py:363
  5.2 0.7 broadcast_in_dim.22.refs_6_
  5.9 0.8 copy.16
  6.7 0.0 collective-permute-done.refs_1_.refs_7_
  6.7 0.0 copy-start
  6.7 1.1 copy-done
  7.8 1.0 copy-done.2
  8.8 0.7 copy-done.4
  9.6 0.7 copy-done.6
  10.2 0.7 copy-done.8
  10.9 0.7 copy-done.10
  11.5 3.9 %shard_map.120 = (bf16[256,1280]{1,0:T(8,128)(2,1)S(1)}, f32[256,1280]{1,0:T(8,128)}, bf16[256,1024]{1,0:T(8,128)(2,1)S(1)}, bf16[256,1024]{1,0:T(8,128)(2,1)S(1)}, bf16[4,64,1152]{2,1,0:T(8,128)(2,1)S(1)}) custom-call(bf16[256,1280]{1,0:T(8,128)(2,1)S(1)} %bitcast.22, bf16[3,1280]{1,0:T(4,128)(2,1)S(1)} %collective-permute-done.refs_1_.refs_7_, ...), custom_call_target="tpu_custom_call" | custom-call | tf_op jit(solution)/shard_map/pallas_call | solution.py:386
  15.5 22.5 %all_to_all.24.near_ref = bf16[4,64,1152]{2,1,0:T(8,128)(2,1)S(1)} all-to-all(bf16[4,64,1152]{2,1,0:T(8,128)(2,1)S(1)} %get-tuple-element.14), channel_id=1, replica_groups=mesh['dp'=4,'ch'=4,'cl'=4,'tp'=8] {'cl'}, dimensions={0} | all-to-all | bytes 1179648 | tf_op jit(solution)/shard_map/all_to_all | solution.py:398
  38.0 0.4 shard_map.121
  38.4 31.5 %all_to_all.25.far_ref = bf16[4,32,1152]{2,1,0:T(8,128)(2,1)S(1)} all-to-all(bf16[4,32,1152]{2,1,0:T(8,128)(2,1)S(1)} %shard_map.121), channel_id=1, replica_groups=mesh['dp'=4,'ch'=4,'cl'=4,'tp'=8] {'ch'}, dimensions={0} | all-to-all | bytes 589824 | tf_op jit(solution)/shard_map/all_to_all | solution.py:400
  69.9 0.0 copy-start.9
  69.9 0.0 copy-start.11
  69.9 0.0 copy-start.12
  70.0 0.6 shard_map.122
  70.5 14.1 %all_to_all.26.refs_0_ = bf16[4,64,1024]{2,1,0:T(8,128)(2,1)S(1)} all-to-all(bf16[4,64,1024]{2,1,0:T(8,128)(2,1)S(1)} %shard_map.122), channel_id=1, replica_groups=mesh['dp'=4,'ch'=4,'cl'=4,'tp'=8] {'cl'}, dimensions={0} | all-to-all | bytes 1048576 | tf_op jit(solution)/shard_map/all_to_all | solution.py:402
  84.6 0.0 copy-done.1
  84.7 7.1 %shard_map.123 = (bf16[256,1280]{1,0:T(8,128)(2,1)}, f32[16,1280]{1,0:T(8,128)S(1)}, f32[8,1280]{1,0:T(8,128)S(1)}, f32[256,16]{1,0:T(8,128)S(1)}, f32[64,128]{1,0:T(8,128)}) custom-call(bf16[4,64,1024]{2,1,0:T(8,128)(2,1)S(1)} %all_to_all.26.refs_0_, bf16[256,1280]{1,0:T(8,128)(2,1)S(1)} %get-tuple-element.15.refs_1_, ...), custom_call_target="tpu_custom_call" | custom-call | tf_op jit(solution)/shard_map/pallas_call | solution.py:404
  91.8 10.2 %all-to-all-start.3 = ((f32[64,1,128]{2,1,0:T(1,128)}), f32[64,1,128]{2,1,0:T(1,128)S(1)}, u32[]{:S(2)}, u32[]{:S(2)}) async-start(f32[64,1,128]{2,1,0:T(1,128)} %bitcast.13), calls=%async_computation.3 | async-start | bytes 65536 | tf_op jit(solution)/shard_map/all_to_all | solution.py:420
  102.0 1.3 %collective-permute-start.1 = (f32[3,1280]{1,0:T(4,128)S(1)}, f32[3,1280]{1,0:T(4,128)S(1)}, u32[]{:S(2)}, u32[]{:S(2)}) collective-permute-start(f32[3,1280]{1,0:T(4,128)S(1)} %slice.33), channel_id=1, source_target_pairs={{8,0},{16,8},{24,16},{32,24},{40,32},{48,40},{56,48},{64,56},{72,6... | collective-permute-start | bytes 46088 | tf_op jit(solution)/shard_map/ppermute | solution.py:363
  103.4 0.7 copy.18
  104.0 3.7 %collective-permute-done.1 = f32[3,1280]{1,0:T(4,128)S(1)} collective-permute-done((f32[3,1280]{1,0:T(4,128)S(1)}, f32[3,1280]{1,0:T(4,128)S(1)}, u32[]{:S(2)}, u32[]{:S(2)}) %collective-permute-start.1) | collective-permute-done | bytes 15392 | tf_op jit(solution)/shard_map/ppermute | solution.py:363
  107.7 0.6 maximum_dynamic-update-slice_fusion
  108.4 7.9 %all-to-all-done.3 = f32[64,1,128]{2,1,0:T(1,128)S(1)} async-done(((f32[64,1,128]{2,1,0:T(1,128)}), f32[64,1,128]{2,1,0:T(1,128)S(1)}, u32[]{:S(2)}, u32[]{:S(2)}) %all-to-all-start.3) | async-done | bytes 32800 | tf_op jit(solution)/shard_map/all_to_all | solution.py:420
  116.3 0.1 reduce_sum.9
  116.4 0.6 slice_bitcast_fusion.1
  117.0 0.7 broadcast_in_dim.27
  (19 shorter events, 0.1 us)
Async XLA Ops:
  1.4 5.3 %collective-permute-start = (bf16[3,1280]{1,0:T(4,128)(2,1)S(1)}, bf16[3,1280]{1,0:T(4,128)(2,1)S(1)}, u32[]{:S(2)}, u32[]{:S(2)}) collective-permute-start(bf16[3,1280]{1,0:T(4,128)(2,1)S(1)} %slice_bitcast_fusion), channel_id=1, source_target_pairs={{0,8},{8,16},{16,24},{24,32},{32,40},{40,48},{48,56},{56,64},{64,7... | collective-permute-start | bytes 23048 | tf_op jit(solution)/shard_map/ppermute | solution.py:363
  6.7 1.1 copy-start
  7.8 1.0 copy-start.2
  8.8 0.7 copy-start.4
  9.5 0.7 copy-start.6
  10.2 0.7 copy-start.8
  10.9 0.7 copy-start.10
  69.9 14.7 %copy-start.1 = (bf16[1,256,1280]{2,1,0:T(8,128)(2,1)S(1)}, bf16[1,256,1280]{2,1,0:T(8,128)(2,1)}, u32[]{:S(2)}) copy-start(bf16[1,256,1280]{2,1,0:T(8,128)(2,1)} %param.9) | copy-start | bytes 1966084
  69.9 14.7 %copy-start.3 = (bf16[1,256,1024]{2,1,0:T(8,128)(2,1)S(1)}, bf16[1,256,1024]{2,1,0:T(8,128)(2,1)}, u32[]{:S(2)}) copy-start(bf16[1,256,1024]{2,1,0:T(8,128)(2,1)} %param.17) | copy-start | bytes 1572868
  69.9 14.7 %copy-start.5 = (bf16[4,1280]{1,0:T(4,128)(2,1)S(1)}, bf16[4,1280]{1,0:T(4,128)(2,1)}, u32[]{:S(2)}) copy-start(bf16[4,1280]{1,0:T(4,128)(2,1)} %refs_11_.1) | copy-start | bytes 30724
  69.9 14.7 %copy-start.7 = (s32[1,256]{1,0:T(1,128)S(1)}, s32[1,256]{1,0:T(1,128)}, u32[]{:S(2)}) copy-start(s32[1,256]{1,0:T(1,128)} %param.11) | copy-start | bytes 3076
  69.9 14.7 %copy-start.9 = (s32[16]{0:T(128)S(1)}, s32[16]{0:T(128)}, u32[]{:S(2)}) copy-start(s32[16]{0:T(128)} %param.12) | copy-start | bytes 196
  69.9 14.7 %copy-start.11 = (f32[16]{0:T(128)S(1)}, f32[16]{0:T(128)}, u32[]{:S(2)}) copy-start(f32[16]{0:T(128)} %param.15) | copy-start | bytes 196
  69.9 14.7 %copy-start.12 = (f32[16]{0:T(128)S(1)}, f32[16]{0:T(128)}, u32[]{:S(2)}) copy-start(f32[16]{0:T(128)} %param.16) | copy-start | bytes 196
  91.8 24.5 %all-to-all-start.3 = ((f32[64,1,128]{2,1,0:T(1,128)}), f32[64,1,128]{2,1,0:T(1,128)S(1)}, u32[]{:S(2)}, u32[]{:S(2)}) async-start(f32[64,1,128]{2,1,0:T(1,128)} %bitcast.13), calls=%async_computation.3 | async-start | bytes 65536 | tf_op jit(solution)/shard_map/all_to_all | solution.py:420
  102.0 5.7 %collective-permute-start.1 = (f32[3,1280]{1,0:T(4,128)S(1)}, f32[3,1280]{1,0:T(4,128)S(1)}, u32[]{:S(2)}, u32[]{:S(2)}) collective-permute-start(f32[3,1280]{1,0:T(4,128)S(1)} %slice.33), channel_id=1, source_target_pairs={{8,0},{16,8},{24,16},{32,24},{40,32},{48,40},{56,48},{64,56},{72,6... | collective-permute-start | bytes 46088 | tf_op jit(solution)/shard_map/ppermute | solution.py:363

commit v3 on v2

v3 whole, which is shorter than its diff:
```python
import math

import jax
import jax.numpy as jnp
from jax import lax
from jax.experimental import pallas as pl
from jax.experimental.pallas import tpu as pltpu
from jax.sharding import PartitionSpec as P

BLOCK = 128
HEAD_WIDTH = 64
STATE = 128
KERNEL = 4
SPLIT = 4
ROWS = STATE // SPLIT
EXTRA = 128
WIDE = 60 * 1024 * 1024
NARROW = 16 * 1024 * 1024
F32 = jnp.float32
BF16 = jnp.bfloat16
CTX = ("ch", "cl")


def mm(left, right):
    return jnp.dot(left, right, preferred_element_type=F32)


def mm_nt(left, right):
    return lax.dot_general(left, right, (((1,), (1,)), ((), ())), preferred_element_type=F32)


def mm_tn(left, right):
    return lax.dot_general(left, right, (((0,), (0,)), ((), ())), preferred_element_type=F32)


def pieces_of(value, count):
    out = []
    for _ in range(count):
        piece = value.astype(BF16)
        out.append(piece)
        value = value - piece.astype(F32)
    return out


def exact_left(ones, value, count):
    return sum(mm(ones, piece) for piece in pieces_of(value, count))


def exact_right(value, ones, count):
    return sum(mm(piece, ones) for piece in pieces_of(value, count))


def spread_matrix(rows, columns):
    row = lax.broadcasted_iota(jnp.int32, (rows, columns), 0)
    lane = lax.broadcasted_iota(jnp.int32, (rows, columns), 1)
    return jnp.where((lane >> 6) == row, 1.0, 0.0).astype(BF16)


def gather_matrix(rows, columns):
    row = lax.broadcasted_iota(jnp.int32, (rows, columns), 0)
    lane = lax.broadcasted_iota(jnp.int32, (rows, columns), 1)
    return jnp.where((row >> 6) == lane, 1.0, 0.0).astype(BF16)


def spread_heads(value, spread, count):
    return sum(mm_tn(piece, spread) for piece in pieces_of(value, count))


def column(line):
    heads = line.shape[1]
    row = lax.broadcasted_iota(jnp.int32, (heads, heads), 0)
    lane = lax.broadcasted_iota(jnp.int32, (heads, heads), 1)
    return jnp.sum(jnp.where(row == lane, line, jnp.zeros_like(line)), axis=1, keepdims=True)


def softplus(value):
    small = jnp.exp(-jnp.abs(value))
    series = small * (1.0 - small * (0.5 - small * (1.0 / 3.0 - small * 0.25)))
    return jnp.maximum(value, 0.0) + jnp.where(small < 0.01, series, jnp.log(1.0 + small))


def triangles():
    row = lax.broadcasted_iota(jnp.int32, (BLOCK, BLOCK), 0)
    lane = lax.broadcasted_iota(jnp.int32, (BLOCK, BLOCK), 1)
    return jnp.where(row >= lane, 1.0, 0.0), jnp.where(row <= lane, 1.0, 0.0)


def block_marks(flags):
    lower, upper = triangles()
    seg_col = jnp.sum(lower * flags, axis=1, keepdims=True)
    seg_row = mm(jnp.broadcast_to(flags, (8, BLOCK)).astype(BF16), upper.astype(BF16))[0:1]
    last = jnp.sum(flags, axis=1, keepdims=True)
    mask = jnp.where(seg_col == seg_row, lower, 0.0)
    alive = jnp.where(seg_col == 0.0, 1.0, 0.0)
    tail = jnp.where(seg_col == last, 1.0, 0.0)
    alive_last = jnp.where(last == 0.0, 1.0, 0.0)
    return mask, alive, tail, alive_last


def head_steps(raw, bias, power, length):
    rate = -0.5 * jnp.exp((power.astype(F32) / 3.0 - 1.0) * math.log(length))
    return softplus(raw + column(bias)), column(rate)


def block_scales(step, rate):
    upper = triangles()[1].astype(BF16)
    cum = exact_right(step * rate, upper, 3)
    total = cum[:, BLOCK - 1 : BLOCK]
    middle = 0.5 * total
    return jnp.exp(cum - middle), step * jnp.exp(middle - cum), jnp.exp(middle), jnp.exp(total)


def wide_lines(half, through, spread):
    lane = lax.broadcasted_iota(jnp.int32, (half.shape[0], 8), 1)
    lines = spread_heads(jnp.where(lane == 0, half, through), spread, 3)
    return lines[0:1], lines[1:2]


def silu_rows(padded, weight, bias_ref, start, cols):
    total = jnp.broadcast_to(bias_ref[:, cols], (64, 128))
    for tap in range(KERNEL):
        at = 8 - (KERNEL - 1) + start + tap
        total = total + padded[at : at + 64, cols] * weight[tap : tap + 1, cols]
    return total, 1.0 / (1.0 + jnp.exp(-total))


def fill_padded(padded, rim, inputs):
    tokens, channels = inputs.shape
    padded[0:8, :] = jnp.zeros((8, channels), F32)
    padded[8 - (KERNEL - 1) : 8, :] = rim.astype(F32)
    padded[8 : 8 + tokens, :] = inputs.astype(F32)


def front_kernel(
    length, input_hbm, rim_hbm, grad_hbm, raw_hbm, flags_hbm, power_hbm, step_bias_hbm, weight_hbm, bias_hbm,
    act_hbm, bx_hbm, ady_hbm, pack_hbm,
    input_ref, rim_ref, grad_ref, raw_ref, flags_ref, power_ref, step_bias_ref, weight_ref, bias_ref,
    act_ref, bx_ref, ady_ref, pack_ref, padded, sems,
):
    pairs = (
        (raw_hbm, raw_ref),
        (step_bias_hbm, step_bias_ref),
        (power_hbm, power_ref),
        (flags_hbm, flags_ref),
        (input_hbm, input_ref),
        (rim_hbm, rim_ref),
        (weight_hbm, weight_ref),
        (bias_hbm, bias_ref),
        (grad_hbm, grad_ref),
        (act_ref, act_hbm),
        (bx_ref, bx_hbm),
        (ady_ref, ady_hbm),
        (pack_ref, pack_hbm),
    )
    copies = [pltpu.make_async_copy(source, target, sems.at[i]) for i, (source, target) in enumerate(pairs)]
    for copy in copies[:9]:
        copy.start()
    tokens, channels = input_ref.shape
    heads = raw_ref.shape[0]
    inner = heads * HEAD_WIDTH
    blocks = tokens // BLOCK
    spread = spread_matrix(heads, inner)
    for copy in copies[:4]:
        copy.wait()
    step, rate = head_steps(raw_ref[...], step_bias_ref[...], power_ref[...], length)
    flags = flags_ref[...].astype(F32)
    marks = [block_marks(flags[block : block + 1]) for block in range(blocks)]
    scales = [block_scales(step[:, block * BLOCK : (block + 1) * BLOCK], rate) for block in range(blocks)]
    for copy in copies[4:8]:
        copy.wait()
    fill_padded(padded, rim_ref[...], input_ref[...])
    weight = weight_ref[...].astype(F32)
    for low in range(0, channels, 128):
        cols = slice(low, low + 128)
        for start in range(0, tokens, 64):
            total, gate = silu_rows(padded, weight, bias_ref, start, cols)
            act_ref[start : start + 64, cols] = (total * gate).astype(BF16)
    copies[9].start()
    copies[8].wait()
    fresh, back, passing = [], [], []
    passing_heads = jnp.ones((heads, 1), F32)
    for block in range(blocks):
        rows = slice(block * BLOCK, (block + 1) * BLOCK)
        _, alive, tail, alive_last = marks[block]
        row_scale, col_scale, half, whole = scales[block]
        through = whole * alive_last
        passing_heads = passing_heads * through
        half_wide, through_wide = wide_lines(half, through, spread)
        bx = (act_ref[rows, 0:inner].astype(F32) * spread_heads(col_scale, spread, 2)).astype(BF16)
        ady = (grad_ref[rows, :].astype(F32) * spread_heads(row_scale, spread, 2)).astype(BF16)
        bx_ref[rows, :] = bx
        ady_ref[rows, :] = ady
        keys = (act_ref[rows, inner : inner + STATE].astype(F32) * tail).astype(BF16)
        queries = (act_ref[rows, inner + STATE : inner + 2 * STATE].astype(F32) * alive).astype(BF16)
        fresh.append(mm_tn(keys, bx) * half_wide)
        back.append(mm_tn(queries, ady) * half_wide)
        passing.append(through_wide)
    copies[10].start()
    copies[11].start()
    up = fresh[0]
    for block in range(1, blocks):
        up = passing[block] * up + fresh[block]
    down = back[blocks - 1]
    for block in range(blocks - 2, -1, -1):
        down = passing[block] * down + back[block]
    pack_ref[:, :, 0:inner] = jnp.concatenate(
        [up.reshape(SPLIT, ROWS, inner), down.reshape(SPLIT, ROWS, inner)], axis=1
    ).astype(BF16)
    row = lax.broadcasted_iota(jnp.int32, (heads, EXTRA), 0)
    lane = lax.broadcasted_iota(jnp.int32, (heads, EXTRA), 1)
    wide = jnp.sum(jnp.where(row == lane, passing_heads, 0.0), axis=0, keepdims=True)
    pack_ref[:, :, inner : inner + EXTRA] = jnp.broadcast_to(
        stacked(wide, 2 * ROWS)[None], (SPLIT, 2 * ROWS, EXTRA)
    )
    copies[12].start()
    for copy in copies[9:]:
        copy.wait()


def stacked(value, rows):
    hi, mid, lo = [piece.astype(F32) for piece in pieces_of(value, 3)]
    line = lax.broadcasted_iota(jnp.int32, (rows, EXTRA), 0)
    return jnp.where(line == 0, hi, jnp.where(line == 1, mid, jnp.where(line == 2, lo, 0.0))).astype(BF16)


def passed(pack_ref, source, inner, spread):
    lines = pack_ref[source, 0:16, inner : inner + EXTRA]
    return (
        jnp.sum(lines.astype(F32), axis=0, keepdims=True),
        jnp.sum(mm(lines, spread), axis=0, keepdims=True),
    )


def totals_kernel(near_ref, out_ref):
    inner = near_ref.shape[2] - EXTRA
    group = lax.axis_index("ch")
    spread = spread_matrix(EXTRA, inner)
    decay = [passed(near_ref, source, inner, spread) for source in range(SPLIT)]
    up = jnp.zeros((ROWS, inner), F32)
    down = jnp.zeros((ROWS, inner), F32)
    through = jnp.ones((1, EXTRA), F32)
    for source in range(SPLIT):
        up = decay[source][1] * up + near_ref[source, 0:ROWS, 0:inner].astype(F32)
        through = through * decay[source][0]
    for source in range(SPLIT - 1, -1, -1):
        down = decay[source][1] * down + near_ref[source, ROWS : 2 * ROWS, 0:inner].astype(F32)
    lines = stacked(through, ROWS)
    for target in range(SPLIT):
        later = jnp.where(target > group, 1.0, 0.0)
        out_ref[target, :, 0:inner] = (later * up + (1.0 - later) * down).astype(BF16)
        out_ref[target, :, inner : inner + EXTRA] = lines


def states_kernel(near_ref, far_ref, out_ref):
    inner = near_ref.shape[2] - EXTRA
    group = lax.axis_index("ch")
    spread = spread_matrix(EXTRA, inner)
    near = [passed(near_ref, source, inner, spread)[1] for source in range(SPLIT)]
    far = [passed(far_ref, source, inner, spread)[1] for source in range(SPLIT)]
    up = jnp.zeros((ROWS, inner), F32)
    down = jnp.zeros((ROWS, inner), F32)
    for source in range(SPLIT):
        use = jnp.where(source < group, 1.0, 0.0)
        up = (use * far[source] + (1.0 - use)) * up + use * far_ref[source, :, 0:inner].astype(F32)
    for source in range(SPLIT - 1, -1, -1):
        use = jnp.where(source > group, 1.0, 0.0)
        down = (use * far[source] + (1.0 - use)) * down + use * far_ref[source, :, 0:inner].astype(F32)
    for source in range(SPLIT):
        out_ref[source, 0:ROWS, :] = up.astype(BF16)
        up = near[source] * up + near_ref[source, 0:ROWS, 0:inner].astype(F32)
    for source in range(SPLIT - 1, -1, -1):
        out_ref[source, ROWS : 2 * ROWS, :] = down.astype(BF16)
        down = near[source] * down + near_ref[source, ROWS : 2 * ROWS, 0:inner].astype(F32)


def local_kernel(
    length, input_ref, rim_ref, grad_ref, raw_ref, flags_ref, power_ref, step_bias_ref, skip_ref, weight_ref, bias_ref,
    act_ref, bx_ref, ady_ref,
    dpre_ref, reach_ref, sums_ref, heads_ref, marked_ref, inside_ref, lines_ref, meets_ref, sides_ref, base_ref,
    padded, slope_ref, product,
):
    tokens, channels = act_ref.shape
    inner = bx_ref.shape[1]
    heads = inner // HEAD_WIDTH
    blocks = tokens // BLOCK
    fill_padded(padded, rim_ref[...], input_ref[...])
    weight = weight_ref[...].astype(F32)
    for low in range(0, channels, 128):
        cols = slice(low, low + 128)
        for start in range(0, tokens, 64):
            total, gate = silu_rows(padded, weight, bias_ref, start, cols)
            slope_ref[start : start + 64, cols] = gate * (1.0 + total * (1.0 - gate))
    step, rate = head_steps(raw_ref[...], step_bias_ref[...], power_ref[...], length)
    heads_ref[0:heads, :] = step
    heads_ref[heads : 2 * heads, :] = 1.0 / (1.0 + jnp.exp(-(raw_ref[...] + column(step_bias_ref[...]))))
    heads_ref[2 * heads : 3 * heads, :] = jnp.broadcast_to(rate, (heads, tokens))
    spread = spread_matrix(heads, inner)
    gather = gather_matrix(inner, heads)
    flags = flags_ref[...].astype(F32)
    skip_wide = spread_heads(jnp.broadcast_to(column(skip_ref[...]), (heads, 8)), spread, 3)[0:1]
    key_cols, query_cols = slice(inner, inner + STATE), slice(inner + STATE, channels)
    for block in range(blocks):
        rows = slice(block * BLOCK, (block + 1) * BLOCK)
        mask, alive, tail, alive_last = block_marks(flags[block : block + 1])
        _, col_scale, half, whole = block_scales(step[:, rows], rate)
        half_wide, through_wide = wide_lines(half, whole * alive_last, spread)
        lines_ref[2 * block : 2 * block + 1, :] = half_wide
        lines_ref[2 * block + 1 : 2 * block + 2, :] = through_wide
        bx = bx_ref[rows, :]
        ady = ady_ref[rows, :]
        key = act_ref[rows, key_cols]
        query = act_ref[rows, query_cols]
        keys = (key.astype(F32) * tail).astype(BF16)
        queries = (query.astype(F32) * alive).astype(BF16)
        marked_ref[rows, 0:STATE] = keys
        marked_ref[rows, STATE : 2 * STATE] = queries
        if block < blocks - 1:
            inside_ref[block] = mm_tn(keys, bx) * half_wide
        if block > 0:
            inside_ref[blocks - 2 + block] = mm_tn(queries, ady) * half_wide
        scores = mask * mm_nt(query, key)
        scores_t = scores.T.astype(BF16)
        dbx = mm(scores_t, ady)
        col_sum = exact_right(bx.astype(F32) * dbx, gather, 2)
        row_sum = exact_right(ady.astype(F32) * mm(scores.astype(BF16), bx), gather, 2)
        sums_ref[0:heads, rows] = (row_sum - col_sum).T
        sums_ref[heads : 2 * heads, rows] = col_sum.T
        dscores = mask * mm_nt(ady, bx)
        dscores_t = dscores.T.astype(BF16)
        dquery = mm(dscores.astype(BF16), key)
        dkey = mm(dscores_t, query)
        slope = slope_ref[rows, 0:inner]
        reach = slope * spread_heads(col_scale, spread, 2)
        reach_ref[rows, 0:inner] = reach
        reach_ref[rows, key_cols] = slope_ref[rows, key_cols] * tail
        reach_ref[rows, query_cols] = slope_ref[rows, query_cols] * alive
        dpre_ref[rows, 0:inner] = reach * dbx + slope * (skip_wide * grad_ref[rows, :].astype(F32))
        dpre_ref[rows, key_cols] = dkey * slope_ref[rows, key_cols]
        dpre_ref[rows, query_cols] = dquery * slope_ref[rows, query_cols]
    lines_ref[2 * blocks :, :] = jnp.zeros((lines_ref.shape[0] - 2 * blocks, inner), F32)
    line = lax.broadcasted_iota(jnp.int32, (8, 128), 0)
    for low in range(0, channels, 128):
        cols = slice(low, low + 128)
        found = jnp.zeros((8, 128), F32)
        for tap in range(KERNEL + 1):
            acc = jnp.zeros((8, 128), F32)
            for start in range(0, tokens, 64):
                rows = slice(start, start + 64)
                at = 8 - (KERNEL - 1) + start + tap
                here, meets = dpre_ref[rows, cols], reach_ref[rows, cols]
                if tap < KERNEL:
                    other = padded[at : at + 64, cols]
                    here, meets = here * other, meets * other
                acc = acc + jnp.sum(here.reshape(8, 8, 128), axis=0)
                if low < inner:
                    product[tap, rows, cols] = meets.astype(BF16)
                else:
                    sides_ref[tap, rows, low - inner : low - inner + 128] = meets.astype(BF16)
            found = jnp.where(line == tap, jnp.sum(acc, axis=0, keepdims=True), found)
        base_ref[:, cols] = found
    line = lax.broadcasted_iota(jnp.int32, (8, inner), 0)
    found = base_ref[:, 0:inner]
    for tap in range(KERNEL + 1):
        through = jnp.ones((1, inner), F32)
        own = jnp.zeros((STATE, inner), F32)
        total = jnp.zeros((STATE, inner), F32)
        for block in range(blocks - 1, -1, -1):
            rows = slice(block * BLOCK, (block + 1) * BLOCK)
            meets = mm_tn(marked_ref[rows, 0:STATE], product[tap, rows, :]) * lines_ref[2 * block : 2 * block + 1, :]
            total = total + through * meets
            if block < blocks - 1:
                found = found + jnp.where(line == tap, jnp.sum(own * meets, axis=0, keepdims=True), 0.0)
            if block > 0:
                decay = lines_ref[2 * block + 1 : 2 * block + 2, :]
                through = decay * through
                own = decay * own + inside_ref[blocks - 2 + block]
        meets_ref[tap] = total.astype(BF16)
    base_ref[:, 0:inner] = found


def block_states(carry_ref, inside_ref, lines_ref, blocks):
    inner = carry_ref.shape[2]
    entering = carry_ref[:, 0:ROWS, :].astype(F32).reshape(STATE, inner)
    leaving = carry_ref[:, ROWS : 2 * ROWS, :].astype(F32).reshape(STATE, inner)
    states, grads = [entering], [leaving]
    for block in range(blocks - 1):
        through = lines_ref[2 * block + 1 : 2 * block + 2, :]
        states.append(through * states[-1] + inside_ref[block])
    for block in range(blocks - 1, 0, -1):
        through = lines_ref[2 * block + 1 : 2 * block + 2, :]
        grads.append(through * grads[-1] + inside_ref[blocks - 2 + block])
    return states, grads[::-1]


def taps_kernel(
    carry_hbm, lines_hbm, inside_hbm, bx_hbm, ady_hbm, marked_hbm, part_hbm, reach_hbm, weight_hbm, meets_hbm, sides_hbm,
    base_hbm,
    head_ref, terms_ref,
    carry_ref, lines_ref, inside_ref, bx_ref, ady_ref, marked_ref, part_ref, reach_ref, weight_ref, meets_ref,
    sides_ref, base_ref, sums_ref, sems,
):
    top = part_ref.shape[0]
    pairs = (
        (carry_hbm, carry_ref),
        (lines_hbm, lines_ref),
        (inside_hbm, inside_ref),
        (bx_hbm, bx_ref),
        (ady_hbm, ady_ref),
        (marked_hbm.at[0:top], marked_ref),
        (part_hbm.at[0:top], part_ref),
        (reach_hbm.at[0:top], reach_ref),
        (weight_hbm, weight_ref),
        (sides_hbm, sides_ref),
        (base_hbm, base_ref),
        (meets_hbm, meets_ref),
    )
    copies = [pltpu.make_async_copy(source, target, sems.at[i]) for i, (source, target) in enumerate(pairs)]
    for copy in copies:
        copy.start()
    channels = part_ref.shape[1]
    tokens, inner = bx_ref.shape
    blocks = tokens // BLOCK
    line = lax.broadcasted_iota(jnp.int32, (8, 128), 0)
    for copy in copies[:9]:
        copy.wait()
    states, grads = block_states(carry_ref, inside_ref, lines_ref, blocks)
    keys, queries = [], []
    for block in range(blocks):
        rows = slice(block * BLOCK, (block + 1) * BLOCK)
        half = lines_ref[2 * block : 2 * block + 1, :]
        grad = (half * grads[block]).astype(BF16)
        keys.append(mm_nt(bx_ref[rows, :], grad))
        queries.append(mm_nt(ady_ref[rows, :], (half * states[block]).astype(BF16)))
        if block == 0:
            first = part_ref[:, 0:inner] + reach_ref[:, 0:inner] * mm(marked_ref[:, 0:STATE], grad)
    key_cols, query_cols = slice(inner, inner + STATE), slice(inner + STATE, channels)
    first = [
        first[0:8],
        (part_ref[:, key_cols] + reach_ref[:, key_cols] * keys[0][0:top])[0:8],
        (part_ref[:, query_cols] + reach_ref[:, query_cols] * queries[0][0:top])[0:8],
    ]
    weight = weight_ref[...].astype(F32)
    for part, cols in zip(first, (slice(0, inner), key_cols, query_cols)):
        wide = lax.broadcasted_iota(jnp.int32, part.shape, 0)
        lines = jnp.zeros(part.shape, F32)
        for at in range(KERNEL - 1):
            row = sum(weight[tap : tap + 1, cols] * part[at - tap : at - tap + 1] for tap in range(at + 1))
            lines = jnp.where(wide == at, row, lines)
        head_ref[:, cols] = lines
    for copy in copies[9:11]:
        copy.wait()
    for side, parts in enumerate((keys, queries)):
        cols = slice(side * STATE, (side + 1) * STATE)
        out = slice(inner + side * STATE, inner + (side + 1) * STATE)
        found = base_ref[:, out]
        for tap in range(KERNEL + 1):
            acc = jnp.zeros((8, STATE), F32)
            for block in range(blocks):
                rows = slice(block * BLOCK, (block + 1) * BLOCK)
                met = parts[block] * sides_ref[tap, rows, cols].astype(F32)
                acc = acc + jnp.sum(met.reshape(BLOCK // 8, 8, STATE), axis=0)
            found = found + jnp.where(line == tap, jnp.sum(acc, axis=0, keepdims=True), 0.0)
        sums_ref[:, out] = found
    copies[11].wait()
    for low in range(0, inner, 128):
        cols = slice(low, low + 128)
        grad = carry_ref[:, ROWS : 2 * ROWS, cols].astype(F32).reshape(STATE, 128)
        found = base_ref[:, cols]
        for tap in range(KERNEL + 1):
            met = grad * meets_ref[tap, :, cols].astype(F32)
            acc = jnp.sum(met.reshape(STATE // 8, 8, 128), axis=0)
            found = found + jnp.where(line == tap, jnp.sum(acc, axis=0, keepdims=True), 0.0)
        sums_ref[:, cols] = found

    targets = terms_ref.shape[0]
    width = channels // targets
    lane = lax.broadcasted_iota(jnp.int32, (8, 128), 1)
    own = (lane >= line * width) & (lane < (line + 1) * width) & (line <= KERNEL)
    for tile in range(channels // 128, sums_ref.shape[1] // 128):
        sums_ref[:, tile * 128 : tile * 128 + 128] = jnp.zeros((8, 128), F32)
    aside = pltpu.roll(sums_ref[...], 0, 1, stride=width // 2, stride_axis=0)
    sums_ref[...] = pltpu.roll(aside, 0, 1, stride=width - width // 2, stride_axis=0)
    for target in range(targets):
        tile, at = divmod(target * width, 128)
        part = sums_ref[:, tile * 128 : tile * 128 + 128]
        if at:
            part = jnp.where(lane >= at, part, sums_ref[:, tile * 128 + 128 : tile * 128 + 256])
            part = pltpu.roll(part, 128 - at, 1)
        terms_ref[target : target + 1, :] = jnp.sum(jnp.where(own, part, 0.0), axis=0, keepdims=True)


def rest_kernel(
    carry_ref, marked_ref, bx_ref, ady_ref, part_ref, reach_ref, inside_ref, lines_ref, sums_ref, heads_ref, weight_ref,
    back_ref,
    out_ref, raw_out_ref, dpre, after,
):
    tokens, channels = part_ref.shape
    inner = bx_ref.shape[1]
    heads = inner // HEAD_WIDTH
    blocks = tokens // BLOCK
    key_cols, query_cols = slice(inner, inner + STATE), slice(inner + STATE, channels)
    gather = gather_matrix(inner, heads)
    lower = triangles()[0].astype(BF16)
    at_last = jnp.where(lax.broadcasted_iota(jnp.int32, (heads, BLOCK), 1) == BLOCK - 1, 1.0, 0.0)
    states, grads = block_states(carry_ref, inside_ref, lines_ref, blocks)
    for block in range(blocks):
        rows = slice(block * BLOCK, (block + 1) * BLOCK)
        half = lines_ref[2 * block : 2 * block + 1, :]
        through = lines_ref[2 * block + 1 : 2 * block + 2, :]
        state = (half * states[block]).astype(BF16)
        grad = (half * grads[block]).astype(BF16)
        keys = marked_ref[rows, 0:STATE]
        queries = marked_ref[rows, STATE : 2 * STATE]
        bx = bx_ref[rows, :]
        ady = ady_ref[rows, :]
        dbx = mm(keys, grad)
        dpre[rows, 0:inner] = part_ref[rows, 0:inner] + reach_ref[rows, 0:inner] * dbx
        dpre[rows, key_cols] = part_ref[rows, key_cols] + reach_ref[rows, key_cols] * mm_nt(bx, grad)
        dpre[rows, query_cols] = part_ref[rows, query_cols] + reach_ref[rows, query_cols] * mm_nt(ady, state)
        row_sum = exact_right(ady.astype(F32) * mm(queries, state), gather, 2)
        col_sum = exact_right(bx.astype(F32) * dbx, gather, 2)
        whole = jnp.sum(
            grad.astype(F32) * mm_tn(keys, bx) + through * (grads[block] * states[block]), axis=0, keepdims=True
        )
        whole = exact_right(jnp.broadcast_to(whole, (8, inner)), gather, 3)
        dcum = sums_ref[0:heads, rows] + (row_sum - col_sum).T + at_last * column(whole[0:1])
        dlog = exact_right(dcum, lower, 3)
        step, gate, rate = (heads_ref[i * heads : (i + 1) * heads, rows] for i in range(3))
        raw_out_ref[:, rows] = ((sums_ref[heads : 2 * heads, rows] + col_sum.T) / step + rate * dlog) * gate
    dpre[tokens : tokens + 8, :] = jnp.zeros((8, channels), F32)
    after[...] = jnp.zeros((8, channels), F32)
    after[8 - (KERNEL - 1) : 8, :] = back_ref[...]
    weight = weight_ref[...].astype(F32)
    for low in range(0, channels, 128):
        cols = slice(low, low + 128)
        for start in range(0, tokens, 64):
            total = dpre[start : start + 64, cols] * weight[KERNEL - 1 : KERNEL, cols]
            for tap in range(KERNEL - 1):
                ahead = start + KERNEL - 1 - tap
                total = total + dpre[ahead : ahead + 64, cols] * weight[tap : tap + 1, cols]
            if start == tokens - 64:
                total = jnp.concatenate([total[0:56], total[56:64] + after[:, cols]], axis=0)
            out_ref[start : start + 64, cols] = total.astype(BF16)


def shares_kernel(scale, terms_ref, weight_ref, bias_ref):
    total = jnp.sum(terms_ref[...], axis=0) * scale
    width = bias_ref.shape[1]
    for tap in range(KERNEL):
        weight_ref[tap, :, :] = total[:, tap * width : (tap + 1) * width]
    bias_ref[...] = total[:, KERNEL * width : (KERNEL + 1) * width]


def call(kernel, out_shape, scratch=(), flops=0, moved=0, vmem=WIDE, **specs):
    return pl.pallas_call(
        kernel,
        out_shape=out_shape,
        scratch_shapes=list(scratch),
        compiler_params=pltpu.CompilerParams(vmem_limit_bytes=vmem),
        cost_estimate=pl.CostEstimate(flops=flops, bytes_accessed=moved, transcendentals=0),
        **specs,
    )


def shifted(value, axis, by):
    devices = lax.axis_size(axis)
    pairs = [(i, i + by) for i in range(devices) if 0 <= i + by < devices]
    return lax.ppermute(value, axis, pairs)


def body(
    conv_input, step_raw, doc_starts, decay_power, conv_weight, conv_bias, step_bias, skip_gain, grad_out
):
    tokens, channels = conv_input.shape[1:]
    heads = step_raw.shape[2]
    inner = heads * HEAD_WIDTH
    ctx_size = lax.axis_size(CTX)
    dp_size = lax.axis_size("dp")
    devices = dp_size * ctx_size
    length = tokens * ctx_size
    inputs = conv_input[0]
    rim = shifted(inputs[tokens - (KERNEL - 1) :], CTX, 1)
    blocks = tokens // BLOCK
    shape = jax.ShapeDtypeStruct
    padded = pltpu.VMEM((tokens + 8, channels), F32)
    placed = pl.BlockSpec(memory_space=pltpu.HBM)
    held = pl.BlockSpec(memory_space=pltpu.VMEM)
    grads = grad_out[0]
    raw = step_raw[0].T
    flags = doc_starts.reshape(blocks, BLOCK)
    power, step_bias, skip, bias = decay_power[None], step_bias[None], skip_gain[None], conv_bias[None]

    def buffers(*arrays):
        return [pltpu.VMEM(array.shape, array.dtype) for array in arrays]

    sources = (inputs, rim, grads, raw, flags, power, step_bias, conv_weight, bias)
    results = (
        shape((tokens, channels), BF16),
        shape((tokens, inner), BF16),
        shape((tokens, inner), BF16),
        shape((SPLIT, 2 * ROWS, inner + EXTRA), BF16),
    )
    act, bx, ady, pack = call(
        lambda *refs: front_kernel(length, *refs),
        results,
        buffers(*sources, *results) + [padded, pltpu.SemaphoreType.DMA((len(sources) + len(results),))],
        in_specs=[placed] * len(sources),
        out_specs=(placed,) * len(results),
    )(*sources)

    part, reach, sums, per_head, marked, inside, lines, meets, sides, base = call(
        lambda *refs: local_kernel(length, *refs),
        (
            shape((tokens, channels), F32),
            shape((tokens, channels), F32),
            shape((2 * heads, tokens), F32),
            shape((3 * heads, tokens), F32),
            shape((tokens, 2 * STATE), BF16),
            shape((2 * (blocks - 1), STATE, inner), F32),
            shape((8, inner), F32),
            shape((KERNEL + 1, STATE, inner), BF16),
            shape((KERNEL + 1, tokens, 2 * STATE), BF16),
            shape((8, channels), F32),
        ),
        [padded, pltpu.VMEM((tokens, channels), F32), pltpu.VMEM((KERNEL + 1, tokens, inner), BF16)],
        flops=10**9,
        moved=10**7,
    )(inputs, rim, grads, raw, flags, power, step_bias, skip, conv_weight, bias, act, bx, ady)

    near = lax.all_to_all(pack, "cl", 0, 0, tiled=True)
    totals = call(totals_kernel, shape((SPLIT, ROWS, inner + EXTRA), BF16), vmem=NARROW)(near)
    far = lax.all_to_all(totals, "ch", 0, 0, tiled=True)
    far, lines = lax.optimization_barrier((far, lines))
    states = call(
        states_kernel,
        shape((SPLIT, 2 * ROWS, inner), BF16),
        vmem=NARROW,
    )(near, far)
    carry = lax.all_to_all(states, "cl", 0, 0, tiled=True)

    sources = (carry, lines, inside, bx, ady, marked, part, reach, conv_weight, meets, sides, base)
    tops = [shape((16,) + a.shape[1:], a.dtype) if a is marked or a is part or a is reach else a for a in sources]
    head, terms = call(
        taps_kernel,
        (shape((8, channels), F32), shape((devices, 128), F32)),
        buffers(*tops) + [pltpu.VMEM((8, channels + 2 * 128), F32), pltpu.SemaphoreType.DMA((len(sources),))],
        in_specs=[placed] * len(sources),
    )(*sources)

    terms = lax.all_to_all(terms.reshape(devices, 1, 128), ("dp",) + CTX, 0, 0, tiled=True)
    back = shifted(head[: KERNEL - 1], CTX, -1)
    out, grad_raw = call(
        rest_kernel,
        (shape((tokens, channels), BF16), shape((heads, tokens), F32)),
        [padded, pltpu.VMEM((8, channels), F32)],
        flops=10**9,
        moved=10**7,
    )(carry, marked, bx, ady, part, reach, inside, lines, sums, per_head, conv_weight, back)
    width = channels // devices
    grad_weight, grad_bias = call(
        lambda *refs: shares_kernel(1.0 / (dp_size * length), *refs),
        (shape((KERNEL, 1, width), F32), shape((1, width), F32)),
        vmem=NARROW,
    )(terms)
    return (out[None], grad_raw.T[None], grad_weight, grad_bias)


def solution(mesh):
    sizes = mesh.shape
    shape = (sizes["dp"], sizes["ctx"] // SPLIT, SPLIT, sizes["tp"])
    mesh = jax.sharding.Mesh(mesh.devices.reshape(shape), ("dp",) + CTX + ("tp",))
    return jax.shard_map(
        body,
        mesh=mesh,
        in_specs=(
            P("dp", CTX, "tp"),
            P("dp", CTX, "tp"),
            P("dp", CTX),
            P("tp"),
            P(None, "tp"),
            P("tp"),
            P("tp"),
            P("tp"),
            P("dp", CTX, "tp"),
        ),
        out_specs=(
            P("dp", CTX, "tp"),
            P("dp", CTX, "tp"),
            P(None, "tp", ("dp",) + CTX),
            P("tp", ("dp",) + CTX),
        ),
        check_vma=False,
    )
```

time: 118 us -> 113 us (0.958)
  blocking collectives: 68.1 us -> 37.8 us
  Pallas kernels: 12 us -> 26.8 us
  starting transfers between devices: 15.3 us -> 27.9 us
  local copies, waits for them, and re-layouts: 9.04 us -> 4.01 us
  waiting for transfers between devices: 11.6 us -> 15.2 us
    all_to_all x1 -> x0, blocking collectives: 31.5 us -> none  [body(): far = lax.all_to_all(totals, 'ch', 0, 0, tiled=True)]
    pallas_call x4 -> x7, Pallas kernels: 12 us -> 26.8 us  [the longest x1 9.46 us: body(): call(lambda *refs: local_kernel(length, *refs), (shape((tokens, channels)...]
    all_to_all x1 -> x2, starting transfers between devices: 10.2 us -> 22.7 us  [the longest x1 12.5 us: body(): far = lax.all_to_all(totals, 'ch', 0, 0, tiled=True)]
    unnamed x28 -> x4, local copies, waits for them, and re-layouts: 6.34 us -> 1.2 us
    all_to_all x1 -> x2, waiting for transfers between devices: 7.94 us -> 10.9 us  [the longest x1 10 us: body(): far = lax.all_to_all(totals, 'ch', 0, 0, tiled=True)]
  transfers between devices with their start and end apart: 3 -> 4, of which waited for: 2 -> 4; matrix products, arithmetic and copies ran while one was open for 2% -> 2% of each run, Pallas kernels for 0% -> 14%
where the time goes in v3:
time: 113 us; the launch traced here: 112 us
  blocking collectives  37.8 us (33%)
  starting transfers between devices  27.9 us (25%)
  Pallas kernels  26.8 us (24%)
  waiting for transfers between devices  15.2 us (13%)
  local copies, waits for them, and re-layouts  4.01 us (4%)
    all_to_all x1, blocking collectives, body(): near = lax.all_to_all(pack, 'cl', 0, 0, tiled=True)  22.7 us
    all_to_all x1, blocking collectives, body(): carry = lax.all_to_all(states, 'cl', 0, 0, tiled=True)  15.1 us
    all_to_all x1, starting transfers between devices, body(): far = lax.all_to_all(totals, 'ch', 0, 0, tiled=True)  12.5 us
    all_to_all x1, starting transfers between devices, body(): lax.all_to_all(terms.reshape(devices, 1, 128), ('dp',) + CTX, 0, 0, tiled...  10.2 us
    all_to_all x1, waiting for transfers between devices, body(): far = lax.all_to_all(totals, 'ch', 0, 0, tiled=True)  10 us
    pallas_call x1, Pallas kernels, body(): call(lambda *refs: local_kernel(length, *refs), (shape((tokens, channels)...  9.46 us
    pallas_call x1, Pallas kernels, body(): call(rest_kernel, (shape((tokens, channels), BF16), shape((heads, tokens)...  6.35 us
    ppermute x2, starting transfers between devices, shifted(): return lax.ppermute(value, axis, pairs)  5.27 us
  transfers between devices with their start and end apart: 4, of which 4 were waited for; matrix products, arithmetic and copies ran while one was open for 2% of the time, Pallas kernels for 14%

profile of v3, /device:TPU:24, one launch (start us, length us, event | category | flops | bytes accessed | tf_op | source)
XLA Modules:
  0.0 112.4 jit_solution(7079596637712405275)
XLA Ops:
  0.6 0.7 slice_bitcast_fusion
  1.4 3.8 %collective-permute-start = (bf16[3,1280]{1,0:T(4,128)(2,1)S(1)}, bf16[3,1280]{1,0:T(4,128)(2,1)S(1)}, u32[]{:S(2)}, u32[]{:S(2)}) collective-permute-start(bf16[3,1280]{1,0:T(4,128)(2,1)S(1)} %slice_bitcast_fusion), channel_id=1, source_target_pairs={{0,8},{8,16},{16,24},{24,32},{32,40},{40,48},{48,56},{56,64},{64,7... | collective-permute-start | bytes 23048 | tf_op jit(solution)/shard_map/ppermute | solution.py:568
  5.2 1.3 %broadcast_in_dim.20.refs_8_.refs_9_ = f32[1,1280]{1,0:T(1,128)} reshape(f32[1280]{0:T(1024)} %param.14) | data formatting | bytes 10240 | tf_op jit(solution)/shard_map/broadcast_in_dim | solution.py:591
  6.5 0.1 collective-permute-done.refs_1_
  6.6 0.0 copy-start.1
  6.6 0.6 copy-done.1
  7.2 4.9 %shard_map.120 = (bf16[256,1280]{1,0:T(8,128)(2,1)}, bf16[256,1024]{1,0:T(8,128)(2,1)}, bf16[256,1024]{1,0:T(8,128)(2,1)}, bf16[4,64,1152]{2,1,0:T(8,128)(2,1)}) custom-call(bf16[256,1280]{1,0:T(8,128)(2,1)} %bitcast.16, bf16[3,1280]{1,0:T(4,128)(2,1)} %copy-done.1, bf16[256,1024]{1,0:T(8,128)(2,1)} %bitcast.18, f32[16,256]{1,0:T(8,128)} %bitcast.21, ...), custom_call_target="tpu_custom_call" | custom-call | tf_op jit(solution)/shard_map/pallas_call | solution.py:603
  12.0 22.7 %all_to_all.20.near_ref = bf16[4,64,1152]{2,1,0:T(8,128)(2,1)S(1)} all-to-all(bf16[4,64,1152]{2,1,0:T(8,128)(2,1)} %get-tuple-element.26), channel_id=1, replica_groups=mesh['dp'=4,'ch'=4,'cl'=4,'tp'=8] {'cl'}, dimensions={0} | all-to-all | bytes 1179648 | tf_op jit(solution)/shard_map/all_to_all | solution.py:630
  34.7 1.1 shard_map.121
  35.8 12.5 %all-to-all-start.1 = ((bf16[4,32,1152]{2,1,0:T(8,128)(2,1)}), bf16[4,32,1152]{2,1,0:T(8,128)(2,1)S(1)}, u32[]{:S(2)}, u32[]{:S(2)}) async-start(bf16[4,32,1152]{2,1,0:T(8,128)(2,1)} %shard_map.121), calls=%async_computation.1 | async-start | bytes 589824 | tf_op jit(solution)/shard_map/all_to_all | solution.py:632
  48.3 9.5 %shard_map.122 = (f32[256,1280]{1,0:T(8,128)}, f32[256,1280]{1,0:T(8,128)}, f32[32,256]{1,0:T(8,128)}, f32[48,256]{1,0:T(8,128)}, bf16[256,256]{1,0:T(8,128)(2,1...) custom-call(bf16[256,1280]{1,0:T(8,128)(2,1)} %bitcast.17, ...), custom_call_target="tpu_custom_call" | custom-call | flops 1000000000 | bytes 10000000 | tf_op jit(solution)/shard_map/pallas_call | solution.py:611
  57.7 10.0 %all-to-all-done.1.far_ref = bf16[4,32,1152]{2,1,0:T(8,128)(2,1)S(1)} async-done(((bf16[4,32,1152]{2,1,0:T(8,128)(2,1)}), bf16[4,32,1152]{2,1,0:T(8,128)(2,1)S(1)}, u32[]{:S(2)}, u32[]{:S(2)}) %all-to-all-start.1) | async-done | bytes 294944 | tf_op jit(solution)/shard_map/all_to_all | solution.py:632
  67.8 0.6 shard_map.123
  68.3 15.1 %all_to_all.21.carry_hbm.carry_ref = bf16[4,64,1024]{2,1,0:T(8,128)(2,1)} all-to-all(bf16[4,64,1024]{2,1,0:T(8,128)(2,1)S(1)} %shard_map.123), channel_id=1, replica_groups=mesh['dp'=4,'ch'=4,'cl'=4,'tp'=8] {'cl'}, dimensions={0} | all-to-all | bytes 1048576 | tf_op jit(solution)/shard_map/all_to_all | solution.py:639
  83.5 3.7 %shard_map.124 = (f32[8,1280]{1,0:T(8,128)}, f32[64,128]{1,0:T(8,128)}) custom-call(bf16[4,64,1024]{2,1,0:T(8,128)(2,1)} %all_to_all.21.carry_hbm.carry_ref, f32[8,1024]{1,0:T(8,128)} %get-tuple-element.36.lines_hbm.lines_ref, f32[2,128,1024]{2,1,0:T(8,128)} %get-tuple-element.35.inside_hbm.inside_ref, ...), custom_call_target="tpu_custom_call" | custom-call | tf_op jit(solution)/shard_map/pallas_call | solution.py:643
  87.2 10.2 %all-to-all-start.3 = ((f32[64,1,128]{2,1,0:T(1,128)}), f32[64,1,128]{2,1,0:T(1,128)S(1)}, u32[]{:S(2)}, u32[]{:S(2)}) async-start(f32[64,1,128]{2,1,0:T(1,128)} %bitcast.20), calls=%async_computation.3 | async-start | bytes 65536 | tf_op jit(solution)/shard_map/all_to_all | solution.py:650
  97.4 0.8 slice.11
  98.2 1.5 %collective-permute-start.1 = (f32[3,1280]{1,0:T(4,128)S(1)}, f32[3,1280]{1,0:T(4,128)S(1)}, u32[]{:S(2)}, u32[]{:S(2)}) collective-permute-start(f32[3,1280]{1,0:T(4,128)S(1)} %slice.11), channel_id=1, source_target_pairs={{8,0},{16,8},{24,16},{32,24},{40,32},{48,40},{56,48},{64,56},{72,6... | collective-permute-start | bytes 46088 | tf_op jit(solution)/shard_map/ppermute | solution.py:568
  99.6 4.2 %collective-permute-done.1.back_ref = f32[3,1280]{1,0:T(4,128)S(1)} collective-permute-done((f32[3,1280]{1,0:T(4,128)S(1)}, f32[3,1280]{1,0:T(4,128)S(1)}, u32[]{:S(2)}, u32[]{:S(2)}) %collective-permute-start.1) | collective-permute-done | bytes 15392 | tf_op jit(solution)/shard_map/ppermute | solution.py:568
  103.8 0.0 copy-start
  103.8 0.6 copy-done
  104.4 6.3 %shard_map.125 = (bf16[256,1280]{1,0:T(8,128)(2,1)}, f32[16,256]{1,0:T(8,128)}) custom-call(bf16[4,64,1024]{2,1,0:T(8,128)(2,1)} %all_to_all.21.carry_hbm.carry_ref, bf16[256,256]{1,0:T(8,128)(2,1)} %get-tuple-element.32.marked_hbm.marked_ref, bf16[256,1024]{1,0:T(8,128)(2,1)} %get-tuple-element.28.refs_11_.bx_hbm.bx_ref, ...), custom_call_target="tpu_custom_call" | custom-call | flops 1000000000 | bytes 10000000 | tf_op jit(solution)/shard_map/pallas_call | solution.py:652
  110.8 0.9 all-to-all-done.3.refs_0_
  111.7 0.7 shard_map.126
Async XLA Ops:
  1.4 5.2 %collective-permute-start = (bf16[3,1280]{1,0:T(4,128)(2,1)S(1)}, bf16[3,1280]{1,0:T(4,128)(2,1)S(1)}, u32[]{:S(2)}, u32[]{:S(2)}) collective-permute-start(bf16[3,1280]{1,0:T(4,128)(2,1)S(1)} %slice_bitcast_fusion), channel_id=1, source_target_pairs={{0,8},{8,16},{16,24},{24,32},{32,40},{40,48},{48,56},{56,64},{64,7... | collective-permute-start | bytes 23048 | tf_op jit(solution)/shard_map/ppermute | solution.py:568
  6.6 0.6 copy-start.1
  35.8 32.0 %all-to-all-start.1 = ((bf16[4,32,1152]{2,1,0:T(8,128)(2,1)}), bf16[4,32,1152]{2,1,0:T(8,128)(2,1)S(1)}, u32[]{:S(2)}, u32[]{:S(2)}) async-start(bf16[4,32,1152]{2,1,0:T(8,128)(2,1)} %shard_map.121), calls=%async_computation.1 | async-start | bytes 589824 | tf_op jit(solution)/shard_map/all_to_all | solution.py:632
  87.2 24.5 %all-to-all-start.3 = ((f32[64,1,128]{2,1,0:T(1,128)}), f32[64,1,128]{2,1,0:T(1,128)S(1)}, u32[]{:S(2)}, u32[]{:S(2)}) async-start(f32[64,1,128]{2,1,0:T(1,128)} %bitcast.20), calls=%async_computation.3 | async-start | bytes 65536 | tf_op jit(solution)/shard_map/all_to_all | solution.py:650
  98.2 5.7 %collective-permute-start.1 = (f32[3,1280]{1,0:T(4,128)S(1)}, f32[3,1280]{1,0:T(4,128)S(1)}, u32[]{:S(2)}, u32[]{:S(2)}) collective-permute-start(f32[3,1280]{1,0:T(4,128)S(1)} %slice.11), channel_id=1, source_target_pairs={{8,0},{16,8},{24,16},{32,24},{40,32},{48,40},{56,48},{64,56},{72,6... | collective-permute-start | bytes 46088 | tf_op jit(solution)/shard_map/ppermute | solution.py:568
  103.8 0.6 copy-start

commit v4 on v3

--- a/solution.py
+++ b/solution.py
@@ -19,6 +19,7 @@
 F32 = jnp.float32
 BF16 = jnp.bfloat16
 CTX = ("ch", "cl")
+NEAR = (2, 1, 0, 3)
 
 
 def mm(left, right):
@@ -203,9 +204,9 @@
     down = back[blocks - 1]
     for block in range(blocks - 2, -1, -1):
         down = passing[block] * down + back[block]
-    pack_ref[:, :, 0:inner] = jnp.concatenate(
-        [up.reshape(SPLIT, ROWS, inner), down.reshape(SPLIT, ROWS, inner)], axis=1
-    ).astype(BF16)
+    for place, source in enumerate(NEAR):
+        rows = slice(source * ROWS, (source + 1) * ROWS)
+        pack_ref[place, :, 0:inner] = jnp.concatenate([up[rows], down[rows]], axis=0).astype(BF16)
     row = lax.broadcasted_iota(jnp.int32, (heads, EXTRA), 0)
     lane = lax.broadcasted_iota(jnp.int32, (heads, EXTRA), 1)
     wide = jnp.sum(jnp.where(row == lane, passing_heads, 0.0), axis=0, keepdims=True)
@@ -231,46 +232,54 @@
     )
 
 
+def near_place(place):
+    return NEAR.index(place)
+
+
+def far_place(group):
+    return (group + SPLIT // 2) % SPLIT
+
+
 def totals_kernel(near_ref, out_ref):
     inner = near_ref.shape[2] - EXTRA
     group = lax.axis_index("ch")
     spread = spread_matrix(EXTRA, inner)
-    decay = [passed(near_ref, source, inner, spread) for source in range(SPLIT)]
+    decay = [passed(near_ref, near_place(source), inner, spread) for source in range(SPLIT)]
     up = jnp.zeros((ROWS, inner), F32)
     down = jnp.zeros((ROWS, inner), F32)
     through = jnp.ones((1, EXTRA), F32)
     for source in range(SPLIT):
-        up = decay[source][1] * up + near_ref[source, 0:ROWS, 0:inner].astype(F32)
+        up = decay[source][1] * up + near_ref[near_place(source), 0:ROWS, 0:inner].astype(F32)
         through = through * decay[source][0]
     for source in range(SPLIT - 1, -1, -1):
-        down = decay[source][1] * down + near_ref[source, ROWS : 2 * ROWS, 0:inner].astype(F32)
+        down = decay[source][1] * down + near_ref[near_place(source), ROWS : 2 * ROWS, 0:inner].astype(F32)
     lines = stacked(through, ROWS)
     for target in range(SPLIT):
         later = jnp.where(target > group, 1.0, 0.0)
-        out_ref[target, :, 0:inner] = (later * up + (1.0 - later) * down).astype(BF16)
-        out_ref[target, :, inner : inner + EXTRA] = lines
+        out_ref[far_place(target), :, 0:inner] = (later * up + (1.0 - later) * down).astype(BF16)
+        out_ref[far_place(target), :, inner : inner + EXTRA] = lines
 
 
 def states_kernel(near_ref, far_ref, out_ref):
     inner = near_ref.shape[2] - EXTRA
     group = lax.axis_index("ch")
     spread = spread_matrix(EXTRA, inner)
-    near = [passed(near_ref, source, inner, spread)[1] for source in range(SPLIT)]
-    far = [passed(far_ref, source, inner, spread)[1] for source in range(SPLIT)]
+    near = [passed(near_ref, near_place(source), inner, spread)[1] for source in range(SPLIT)]
+    far = [passed(far_ref, far_place(source), inner, spread)[1] for source in range(SPLIT)]
     up = jnp.zeros((ROWS, inner), F32)
     down = jnp.zeros((ROWS, inner), F32)
     for source in range(SPLIT):
         use = jnp.where(source < group, 1.0, 0.0)
-        up = (use * far[source] + (1.0 - use)) * up + use * far_ref[source, :, 0:inner].astype(F32)
+        up = (use * far[source] + (1.0 - use)) * up + use * far_ref[far_place(source), :, 0:inner].astype(F32)
     for source in range(SPLIT - 1, -1, -1):
         use = jnp.where(source > group, 1.0, 0.0)
-        down = (use * far[source] + (1.0 - use)) * down + use * far_ref[source, :, 0:inner].astype(F32)
+        down = (use * far[source] + (1.0 - use)) * down + use * far_ref[far_place(source), :, 0:inner].astype(F32)
     for source in range(SPLIT):
-        out_ref[source, 0:ROWS, :] = up.astype(BF16)
-        up = near[source] * up + near_ref[source, 0:ROWS, 0:inner].astype(F32)
+        out_ref[near_place(source), 0:ROWS, :] = up.astype(BF16)
+        up = near[source] * up + near_ref[near_place(source), 0:ROWS, 0:inner].astype(F32)
     for source in range(SPLIT - 1, -1, -1):
-        out_ref[source, ROWS : 2 * ROWS, :] = down.astype(BF16)
-        down = near[source] * down + near_ref[source, ROWS : 2 * ROWS, 0:inner].astype(F32)
+        out_ref[near_place(source), ROWS : 2 * ROWS, :] = down.astype(BF16)
+        down = near[source] * down + near_ref[near_place(source), ROWS : 2 * ROWS, 0:inner].astype(F32)
 
 
 def local_kernel(
@@ -379,9 +388,10 @@
 
 
 def block_states(carry_ref, inside_ref, lines_ref, blocks):
-    inner = carry_ref.shape[2]
-    entering = carry_ref[:, 0:ROWS, :].astype(F32).reshape(STATE, inner)
-    leaving = carry_ref[:, ROWS : 2 * ROWS, :].astype(F32).reshape(STATE, inner)
+    entering, leaving = (
+        jnp.concatenate([carry_ref[near_place(i), low : low + ROWS, :].astype(F32) for i in range(SPLIT)], axis=0)
+        for low in (0, ROWS)
+    )
     states, grads = [entering], [leaving]
     for block in range(blocks - 1):
         through = lines_ref[2 * block + 1 : 2 * block + 2, :]
@@ -464,7 +474,9 @@
     copies[11].wait()
     for low in range(0, inner, 128):
         cols = slice(low, low + 128)
-        grad = carry_ref[:, ROWS : 2 * ROWS, cols].astype(F32).reshape(STATE, 128)
+        grad = jnp.concatenate(
+            [carry_ref[near_place(i), ROWS : 2 * ROWS, cols].astype(F32) for i in range(SPLIT)], axis=0
+        )
         found = base_ref[:, cols]
         for tap in range(KERNEL + 1):
             met = grad * meets_ref[tap, :, cols].astype(F32)
@@ -627,16 +639,17 @@
         moved=10**7,
     )(inputs, rim, grads, raw, flags, power, step_bias, skip, conv_weight, bias, act, bx, ady)
 
-    near = lax.all_to_all(pack, "cl", 0, 0, tiled=True)
+    near = lax.all_to_all(pack, "cl", 0, 0, tiled=True, axis_index_groups=[list(NEAR)])
     totals = call(totals_kernel, shape((SPLIT, ROWS, inner + EXTRA), BF16), vmem=NARROW)(near)
-    far = lax.all_to_all(totals, "ch", 0, 0, tiled=True)
+    turned = [[far_place(place) for place in range(SPLIT)]]
+    far = lax.all_to_all(totals, "ch", 0, 0, tiled=True, axis_index_groups=turned)
     far, lines = lax.optimization_barrier((far, lines))
     states = call(
         states_kernel,
         shape((SPLIT, 2 * ROWS, inner), BF16),
         vmem=NARROW,
     )(near, far)
-    carry = lax.all_to_all(states, "cl", 0, 0, tiled=True)
+    carry = lax.all_to_all(states, "cl", 0, 0, tiled=True, axis_index_groups=[list(NEAR)])
 
     sources = (carry, lines, inside, bx, ady, marked, part, reach, conv_weight, meets, sides, base)
     tops = [shape((16,) + a.shape[1:], a.dtype) if a is marked or a is part or a is reach else a for a in sources]

time: 113 us -> 107 us (0.947)
  waiting for transfers between devices: 15.2 us -> 5.23 us
  starting transfers between devices: 27.9 us -> 32.6 us
    all_to_all x1, waiting for transfers between devices: 10 us -> 0.08 us  [body(): lax.all_to_all(totals, 'ch', 0, 0, tiled=True, axis_index_groups=turned)]
    all_to_all x1, starting transfers between devices: 10.2 us -> 12.5 us  [body(): lax.all_to_all(terms.reshape(devices, 1, 128), ('dp',) + CTX, 0, 0, tiled...]
    all_to_all x1, starting transfers between devices: 12.5 us -> 14.8 us  [body(): lax.all_to_all(totals, 'ch', 0, 0, tiled=True, axis_index_groups=turned)]
  transfers between devices with their start and end apart: 4 -> 4, of which waited for: 4 -> 4; matrix products, arithmetic and copies ran while one was open for 2% -> 2% of each run, Pallas kernels for 14% -> 15%
where the time goes in v4:
time: 107 us; the launch traced here: 106 us
  blocking collectives  37 us (35%)
  starting transfers between devices  32.6 us (30%)
  Pallas kernels  26.8 us (25%)
  waiting for transfers between devices  5.23 us (5%)
  local copies, waits for them, and re-layouts  4.01 us (4%)
    all_to_all x1, blocking collectives, body(): lax.all_to_all(pack, 'cl', 0, 0, tiled=True, axis_index_groups=[list(NEAR)])  20.6 us
    all_to_all x1, blocking collectives, body(): lax.all_to_all(states, 'cl', 0, 0, tiled=True, axis_index_groups=[list(NE...  16.4 us
    all_to_all x1, starting transfers between devices, body(): lax.all_to_all(totals, 'ch', 0, 0, tiled=True, axis_index_groups=turned)  14.8 us
    all_to_all x1, starting transfers between devices, body(): lax.all_to_all(terms.reshape(devices, 1, 128), ('dp',) + CTX, 0, 0, tiled...  12.5 us
    pallas_call x1, Pallas kernels, body(): call(lambda *refs: local_kernel(length, *refs), (shape((tokens, channels)...  9.46 us
    pallas_call x1, Pallas kernels, body(): call(rest_kernel, (shape((tokens, channels), BF16), shape((heads, tokens)...  6.34 us
    ppermute x2, starting transfers between devices, shifted(): return lax.ppermute(value, axis, pairs)  5.27 us
    pallas_call x1, Pallas kernels, body(): call(lambda *refs: front_kernel(length, *refs), results, buffers(*sources...  4.85 us
  transfers between devices with their start and end apart: 4, of which 4 were waited for; matrix products, arithmetic and copies ran while one was open for 2% of the time, Pallas kernels for 15%

profile of v4, /device:TPU:24, one launch (start us, length us, event | category | flops | bytes accessed | tf_op | source)
XLA Modules:
  0.0 106.3 jit_solution(6135197831557136585)
XLA Ops:
  0.6 0.7 slice_bitcast_fusion
  1.4 3.8 %collective-permute-start = (bf16[3,1280]{1,0:T(4,128)(2,1)S(1)}, bf16[3,1280]{1,0:T(4,128)(2,1)S(1)}, u32[]{:S(2)}, u32[]{:S(2)}) collective-permute-start(bf16[3,1280]{1,0:T(4,128)(2,1)S(1)} %slice_bitcast_fusion), channel_id=1, source_target_pairs={{0,8},{8,16},{16,24},{24,32},{32,40},{40,48},{48,56},{56,64},{64,7... | collective-permute-start | bytes 23048 | tf_op jit(solution)/shard_map/ppermute | solution.py:580
  5.2 1.3 %broadcast_in_dim.20.refs_8_.refs_9_ = f32[1,1280]{1,0:T(1,128)} reshape(f32[1280]{0:T(1024)} %param.14) | data formatting | bytes 10240 | tf_op jit(solution)/shard_map/broadcast_in_dim | solution.py:603
  6.5 0.1 collective-permute-done.refs_1_
  6.6 0.0 copy-start.1
  6.6 0.6 copy-done.1
  7.2 4.9 %shard_map.120 = (bf16[256,1280]{1,0:T(8,128)(2,1)}, bf16[256,1024]{1,0:T(8,128)(2,1)}, bf16[256,1024]{1,0:T(8,128)(2,1)}, bf16[4,64,1152]{2,1,0:T(8,128)(2,1)}) custom-call(bf16[256,1280]{1,0:T(8,128)(2,1)} %bitcast.16, bf16[3,1280]{1,0:T(4,128)(2,1)} %copy-done.1, bf16[256,1024]{1,0:T(8,128)(2,1)} %bitcast.18, f32[16,256]{1,0:T(8,128)} %bitcast.21, ...), custom_call_target="tpu_custom_call" | custom-call | tf_op jit(solution)/shard_map/pallas_call | solution.py:615
  12.0 20.6 %all_to_all.20.near_ref = bf16[4,64,1152]{2,1,0:T(8,128)(2,1)S(1)} all-to-all(bf16[4,64,1152]{2,1,0:T(8,128)(2,1)} %get-tuple-element.26), channel_id=1, replica_groups={{16,8,0,24},{17,9,1,25},{18,10,2,26},{19,11,3,27},{20,12,4,28},{21,13,5..., dimensions={0} | all-to-all | bytes 1179648 | tf_op jit(solution)/shard_map/all_to_all | solution.py:642
  32.6 1.1 %shard_map.121 = bf16[4,32,1152]{2,1,0:T(8,128)(2,1)} custom-call(bf16[4,64,1152]{2,1,0:T(8,128)(2,1)S(1)} %all_to_all.20.near_ref), custom_call_target="tpu_custom_call" | custom-call | tf_op jit(solution)/shard_map/pallas_call | solution.py:643
  33.7 14.8 %all-to-all-start.1 = ((bf16[4,32,1152]{2,1,0:T(8,128)(2,1)}), bf16[4,32,1152]{2,1,0:T(8,128)(2,1)S(1)}, u32[]{:S(2)}, u32[]{:S(2)}) async-start(bf16[4,32,1152]{2,1,0:T(8,128)(2,1)} %shard_map.121), calls=%async_computation.1 | async-start | bytes 589824 | tf_op jit(solution)/shard_map/all_to_all | solution.py:645
  48.5 9.5 %shard_map.122 = (f32[256,1280]{1,0:T(8,128)}, f32[256,1280]{1,0:T(8,128)}, f32[32,256]{1,0:T(8,128)}, f32[48,256]{1,0:T(8,128)}, bf16[256,256]{1,0:T(8,128)(2,1...) custom-call(bf16[256,1280]{1,0:T(8,128)(2,1)} %bitcast.17, ...), custom_call_target="tpu_custom_call" | custom-call | flops 1000000000 | bytes 10000000 | tf_op jit(solution)/shard_map/pallas_call | solution.py:623
  57.9 0.1 all-to-all-done.1.far_ref
  58.0 0.6 shard_map.123
  58.6 16.4 %all_to_all.21.carry_hbm.carry_ref = bf16[4,64,1024]{2,1,0:T(8,128)(2,1)} all-to-all(bf16[4,64,1024]{2,1,0:T(8,128)(2,1)S(1)} %shard_map.123), channel_id=1, replica_groups={{16,8,0,24},{17,9,1,25},{18,10,2,26},{19,11,3,27},{20,12,4,28},{21,13,5..., dimensions={0} | all-to-all | bytes 1048576 | tf_op jit(solution)/shard_map/all_to_all | solution.py:652
  75.0 3.7 %shard_map.124 = (f32[8,1280]{1,0:T(8,128)}, f32[64,128]{1,0:T(8,128)}) custom-call(bf16[4,64,1024]{2,1,0:T(8,128)(2,1)} %all_to_all.21.carry_hbm.carry_ref, f32[8,1024]{1,0:T(8,128)} %get-tuple-element.36.lines_hbm.lines_ref, f32[2,128,1024]{2,1,0:T(8,128)} %get-tuple-element.35.inside_hbm.inside_ref, ...), custom_call_target="tpu_custom_call" | custom-call | tf_op jit(solution)/shard_map/pallas_call | solution.py:656
  78.7 12.5 %all-to-all-start.3 = ((f32[64,1,128]{2,1,0:T(1,128)}), f32[64,1,128]{2,1,0:T(1,128)S(1)}, u32[]{:S(2)}, u32[]{:S(2)}) async-start(f32[64,1,128]{2,1,0:T(1,128)} %bitcast.20), calls=%async_computation.3 | async-start | bytes 65536 | tf_op jit(solution)/shard_map/all_to_all | solution.py:663
  91.3 0.8 slice.11
  92.0 1.5 %collective-permute-start.1 = (f32[3,1280]{1,0:T(4,128)S(1)}, f32[3,1280]{1,0:T(4,128)S(1)}, u32[]{:S(2)}, u32[]{:S(2)}) collective-permute-start(f32[3,1280]{1,0:T(4,128)S(1)} %slice.11), channel_id=1, source_target_pairs={{8,0},{16,8},{24,16},{32,24},{40,32},{48,40},{56,48},{64,56},{72,6... | collective-permute-start | bytes 46088 | tf_op jit(solution)/shard_map/ppermute | solution.py:580
  93.5 4.2 %collective-permute-done.1.back_ref = f32[3,1280]{1,0:T(4,128)S(1)} collective-permute-done((f32[3,1280]{1,0:T(4,128)S(1)}, f32[3,1280]{1,0:T(4,128)S(1)}, u32[]{:S(2)}, u32[]{:S(2)}) %collective-permute-start.1) | collective-permute-done | bytes 15392 | tf_op jit(solution)/shard_map/ppermute | solution.py:580
  97.7 0.0 copy-start
  97.7 0.6 copy-done
  98.3 6.3 %shard_map.125 = (bf16[256,1280]{1,0:T(8,128)(2,1)}, f32[16,256]{1,0:T(8,128)}) custom-call(bf16[4,64,1024]{2,1,0:T(8,128)(2,1)} %all_to_all.21.carry_hbm.carry_ref, bf16[256,256]{1,0:T(8,128)(2,1)} %get-tuple-element.32.marked_hbm.marked_ref, bf16[256,1024]{1,0:T(8,128)(2,1)} %get-tuple-element.28.refs_11_.bx_hbm.bx_ref, ...), custom_call_target="tpu_custom_call" | custom-call | flops 1000000000 | bytes 10000000 | tf_op jit(solution)/shard_map/pallas_call | solution.py:665
  104.7 0.9 all-to-all-done.3.refs_0_
  105.5 0.7 shard_map.126
Async XLA Ops:
  1.4 5.2 %collective-permute-start = (bf16[3,1280]{1,0:T(4,128)(2,1)S(1)}, bf16[3,1280]{1,0:T(4,128)(2,1)S(1)}, u32[]{:S(2)}, u32[]{:S(2)}) collective-permute-start(bf16[3,1280]{1,0:T(4,128)(2,1)S(1)} %slice_bitcast_fusion), channel_id=1, source_target_pairs={{0,8},{8,16},{16,24},{24,32},{32,40},{40,48},{48,56},{56,64},{64,7... | collective-permute-start | bytes 23048 | tf_op jit(solution)/shard_map/ppermute | solution.py:580
  6.6 0.6 copy-start.1
  33.7 24.3 %all-to-all-start.1 = ((bf16[4,32,1152]{2,1,0:T(8,128)(2,1)}), bf16[4,32,1152]{2,1,0:T(8,128)(2,1)S(1)}, u32[]{:S(2)}, u32[]{:S(2)}) async-start(bf16[4,32,1152]{2,1,0:T(8,128)(2,1)} %shard_map.121), calls=%async_computation.1 | async-start | bytes 589824 | tf_op jit(solution)/shard_map/all_to_all | solution.py:645
  78.7 26.8 %all-to-all-start.3 = ((f32[64,1,128]{2,1,0:T(1,128)}), f32[64,1,128]{2,1,0:T(1,128)S(1)}, u32[]{:S(2)}, u32[]{:S(2)}) async-start(f32[64,1,128]{2,1,0:T(1,128)} %bitcast.20), calls=%async_computation.3 | async-start | bytes 65536 | tf_op jit(solution)/shard_map/all_to_all | solution.py:663
  92.0 5.7 %collective-permute-start.1 = (f32[3,1280]{1,0:T(4,128)S(1)}, f32[3,1280]{1,0:T(4,128)S(1)}, u32[]{:S(2)}, u32[]{:S(2)}) collective-permute-start(f32[3,1280]{1,0:T(4,128)S(1)} %slice.11), channel_id=1, source_target_pairs={{8,0},{16,8},{24,16},{32,24},{40,32},{48,40},{56,48},{64,56},{72,6... | collective-permute-start | bytes 46088 | tf_op jit(solution)/shard_map/ppermute | solution.py:580
  97.7 0.6 copy-start

commit v5 on v4

--- a/solution.py
+++ b/solution.py
@@ -640,10 +640,10 @@
     )(inputs, rim, grads, raw, flags, power, step_bias, skip, conv_weight, bias, act, bx, ady)
 
     near = lax.all_to_all(pack, "cl", 0, 0, tiled=True, axis_index_groups=[list(NEAR)])
+    near, lines = lax.optimization_barrier((near, lines))
     totals = call(totals_kernel, shape((SPLIT, ROWS, inner + EXTRA), BF16), vmem=NARROW)(near)
     turned = [[far_place(place) for place in range(SPLIT)]]
     far = lax.all_to_all(totals, "ch", 0, 0, tiled=True, axis_index_groups=turned)
-    far, lines = lax.optimization_barrier((far, lines))
     states = call(
         states_kernel,
         shape((SPLIT, 2 * ROWS, inner), BF16),

time: 107 us -> 104 us (0.972)
  starting transfers between devices: 32.6 us -> 26.2 us
  waiting for transfers between devices: 5.23 us -> 8.75 us
    all_to_all x1, starting transfers between devices: 14.8 us -> 7.68 us  [body(): lax.all_to_all(pack, 'cl', 0, 0, tiled=True, axis_index_groups=[list(NEAR)])]
    all_to_all x1, blocking collectives: 20.6 us -> 25.5 us  [body(): lax.all_to_all(totals, 'ch', 0, 0, tiled=True, axis_index_groups=turned)]
    all_to_all x1, blocking collectives: 16.4 us -> 12.2 us  [body(): lax.all_to_all(states, 'cl', 0, 0, tiled=True, axis_index_groups=[list(NE...]
    all_to_all x1, waiting for transfers between devices: 0.08 us -> 3.47 us  [body(): lax.all_to_all(pack, 'cl', 0, 0, tiled=True, axis_index_groups=[list(NEAR)])]
where the time goes in v5:
time: 104 us; the launch traced here: 103 us
  blocking collectives  37.7 us (36%)
  starting transfers between devices  26.2 us (25%)
  Pallas kernels  26 us (25%)
  waiting for transfers between devices  8.75 us (8%)
  local copies, waits for them, and re-layouts  4.02 us (4%)
    all_to_all x1, blocking collectives, body(): lax.all_to_all(totals, 'ch', 0, 0, tiled=True, axis_index_groups=turned)  25.5 us
    all_to_all x1, starting transfers between devices, body(): lax.all_to_all(terms.reshape(devices, 1, 128), ('dp',) + CTX, 0, 0, tiled...  13.2 us
    all_to_all x1, blocking collectives, body(): lax.all_to_all(states, 'cl', 0, 0, tiled=True, axis_index_groups=[list(NE...  12.2 us
    pallas_call x1, Pallas kernels, body(): call(lambda *refs: local_kernel(length, *refs), (shape((tokens, channels)...  9.44 us
    all_to_all x1, starting transfers between devices, body(): lax.all_to_all(pack, 'cl', 0, 0, tiled=True, axis_index_groups=[list(NEAR)])  7.68 us
    pallas_call x1, Pallas kernels, body(): call(rest_kernel, (shape((tokens, channels), BF16), shape((heads, tokens)...  6.34 us
    ppermute x2, starting transfers between devices, shifted(): return lax.ppermute(value, axis, pairs)  5.27 us
    pallas_call x1, Pallas kernels, body(): call(lambda *refs: front_kernel(length, *refs), results, buffers(*sources...  4.83 us
  transfers between devices with their start and end apart: 4, of which 4 were waited for; matrix products, arithmetic and copies ran while one was open for 2% of the time, Pallas kernels for 15%

profile of v5, /device:TPU:24, one launch (start us, length us, event | category | flops | bytes accessed | tf_op | source)
XLA Modules:
  0.0 103.3 jit_solution(10777443573922139380)
XLA Ops:
  0.6 0.7 slice_bitcast_fusion
  1.4 3.8 %collective-permute-start = (bf16[3,1280]{1,0:T(4,128)(2,1)S(1)}, bf16[3,1280]{1,0:T(4,128)(2,1)S(1)}, u32[]{:S(2)}, u32[]{:S(2)}) collective-permute-start(bf16[3,1280]{1,0:T(4,128)(2,1)S(1)} %slice_bitcast_fusion), channel_id=1, source_target_pairs={{0,8},{8,16},{16,24},{24,32},{32,40},{40,48},{48,56},{56,64},{64,7... | collective-permute-start | bytes 23048 | tf_op jit(solution)/shard_map/ppermute | solution.py:580
  5.2 1.3 %broadcast_in_dim.20.refs_8_.refs_9_ = f32[1,1280]{1,0:T(1,128)} reshape(f32[1280]{0:T(1024)} %param.14) | data formatting | bytes 10240 | tf_op jit(solution)/shard_map/broadcast_in_dim | solution.py:603
  6.5 0.1 collective-permute-done.refs_1_
  6.6 0.0 copy-start.1
  6.6 0.6 copy-done.1
  7.2 4.8 %shard_map.120 = (bf16[256,1280]{1,0:T(8,128)(2,1)}, bf16[256,1024]{1,0:T(8,128)(2,1)}, bf16[256,1024]{1,0:T(8,128)(2,1)}, bf16[4,64,1152]{2,1,0:T(8,128)(2,1)}) custom-call(bf16[256,1280]{1,0:T(8,128)(2,1)} %bitcast.16, bf16[3,1280]{1,0:T(4,128)(2,1)} %copy-done.1, bf16[256,1024]{1,0:T(8,128)(2,1)} %bitcast.18, f32[16,256]{1,0:T(8,128)} %bitcast.21, ...), custom_call_target="tpu_custom_call" | custom-call | tf_op jit(solution)/shard_map/pallas_call | solution.py:615
  12.0 7.7 %all-to-all-start = ((bf16[4,64,1152]{2,1,0:T(8,128)(2,1)}), bf16[4,64,1152]{2,1,0:T(8,128)(2,1)S(1)}, u32[]{:S(2)}, u32[]{:S(2)}) async-start(bf16[4,64,1152]{2,1,0:T(8,128)(2,1)} %get-tuple-element.26), calls=%async_computation | async-start | bytes 1179648 | tf_op jit(solution)/shard_map/all_to_all | solution.py:642
  19.7 9.4 %shard_map.121 = (f32[256,1280]{1,0:T(8,128)}, f32[256,1280]{1,0:T(8,128)}, f32[32,256]{1,0:T(8,128)}, f32[48,256]{1,0:T(8,128)}, bf16[256,256]{1,0:T(8,128)(2,1...) custom-call(bf16[256,1280]{1,0:T(8,128)(2,1)} %bitcast.17, ...), custom_call_target="tpu_custom_call" | custom-call | flops 1000000000 | bytes 10000000 | tf_op jit(solution)/shard_map/pallas_call | solution.py:623
  29.1 3.5 %all-to-all-done.near_ref = bf16[4,64,1152]{2,1,0:T(8,128)(2,1)S(1)} async-done(((bf16[4,64,1152]{2,1,0:T(8,128)(2,1)}), bf16[4,64,1152]{2,1,0:T(8,128)(2,1)S(1)}, u32[]{:S(2)}, u32[]{:S(2)}) %all-to-all-start) | async-done | bytes 589856 | tf_op jit(solution)/shard_map/all_to_all | solution.py:642
  32.6 0.4 shard_map.122
  33.0 25.5 %all_to_all.20.far_ref = bf16[4,32,1152]{2,1,0:T(8,128)(2,1)S(1)} all-to-all(bf16[4,32,1152]{2,1,0:T(8,128)(2,1)S(1)} %shard_map.122), channel_id=1, replica_groups={{64,96,0,32},{65,97,1,33},{66,98,2,34},{67,99,3,35},{68,100,4,36},{69,1..., dimensions={0} | all-to-all | bytes 589824 | tf_op jit(solution)/shard_map/all_to_all | solution.py:646
  58.5 0.6 shard_map.123
  59.0 12.2 %all_to_all.21.carry_hbm.carry_ref = bf16[4,64,1024]{2,1,0:T(8,128)(2,1)} all-to-all(bf16[4,64,1024]{2,1,0:T(8,128)(2,1)S(1)} %shard_map.123), channel_id=1, replica_groups={{16,8,0,24},{17,9,1,25},{18,10,2,26},{19,11,3,27},{20,12,4,28},{21,13,5..., dimensions={0} | all-to-all | bytes 1048576 | tf_op jit(solution)/shard_map/all_to_all | solution.py:652
  71.2 3.7 %shard_map.124 = (f32[8,1280]{1,0:T(8,128)}, f32[64,128]{1,0:T(8,128)}) custom-call(bf16[4,64,1024]{2,1,0:T(8,128)(2,1)} %all_to_all.21.carry_hbm.carry_ref, f32[8,1024]{1,0:T(8,128)} %get-tuple-element.36.lines_hbm.lines_ref, f32[2,128,1024]{2,1,0:T(8,128)} %get-tuple-element.35.inside_hbm.inside_ref, ...), custom_call_target="tpu_custom_call" | custom-call | tf_op jit(solution)/shard_map/pallas_call | solution.py:656
  74.9 13.2 %all-to-all-start.3 = ((f32[64,1,128]{2,1,0:T(1,128)}), f32[64,1,128]{2,1,0:T(1,128)S(1)}, u32[]{:S(2)}, u32[]{:S(2)}) async-start(f32[64,1,128]{2,1,0:T(1,128)} %bitcast.20), calls=%async_computation.3 | async-start | bytes 65536 | tf_op jit(solution)/shard_map/all_to_all | solution.py:663
  88.2 0.8 slice.11
  88.9 1.5 %collective-permute-start.1 = (f32[3,1280]{1,0:T(4,128)S(1)}, f32[3,1280]{1,0:T(4,128)S(1)}, u32[]{:S(2)}, u32[]{:S(2)}) collective-permute-start(f32[3,1280]{1,0:T(4,128)S(1)} %slice.11), channel_id=1, source_target_pairs={{8,0},{16,8},{24,16},{32,24},{40,32},{48,40},{56,48},{64,56},{72,6... | collective-permute-start | bytes 46088 | tf_op jit(solution)/shard_map/ppermute | solution.py:580
  90.4 4.2 %collective-permute-done.1.back_ref = f32[3,1280]{1,0:T(4,128)S(1)} collective-permute-done((f32[3,1280]{1,0:T(4,128)S(1)}, f32[3,1280]{1,0:T(4,128)S(1)}, u32[]{:S(2)}, u32[]{:S(2)}) %collective-permute-start.1) | collective-permute-done | bytes 15392 | tf_op jit(solution)/shard_map/ppermute | solution.py:580
  94.6 0.0 copy-start
  94.6 0.6 copy-done
  95.2 6.3 %shard_map.125 = (bf16[256,1280]{1,0:T(8,128)(2,1)}, f32[16,256]{1,0:T(8,128)}) custom-call(bf16[4,64,1024]{2,1,0:T(8,128)(2,1)} %all_to_all.21.carry_hbm.carry_ref, bf16[256,256]{1,0:T(8,128)(2,1)} %get-tuple-element.32.marked_hbm.marked_ref, bf16[256,1024]{1,0:T(8,128)(2,1)} %get-tuple-element.28.refs_11_.bx_hbm.bx_ref, ...), custom_call_target="tpu_custom_call" | custom-call | flops 1000000000 | bytes 10000000 | tf_op jit(solution)/shard_map/pallas_call | solution.py:665
  101.6 1.0 all-to-all-done.3.refs_0_
  102.6 0.7 shard_map.126
Async XLA Ops:
  1.4 5.2 %collective-permute-start = (bf16[3,1280]{1,0:T(4,128)(2,1)S(1)}, bf16[3,1280]{1,0:T(4,128)(2,1)S(1)}, u32[]{:S(2)}, u32[]{:S(2)}) collective-permute-start(bf16[3,1280]{1,0:T(4,128)(2,1)S(1)} %slice_bitcast_fusion), channel_id=1, source_target_pairs={{0,8},{8,16},{16,24},{24,32},{32,40},{40,48},{48,56},{56,64},{64,7... | collective-permute-start | bytes 23048 | tf_op jit(solution)/shard_map/ppermute | solution.py:580
  6.6 0.6 copy-start.1
  12.0 20.6 %all-to-all-start = ((bf16[4,64,1152]{2,1,0:T(8,128)(2,1)}), bf16[4,64,1152]{2,1,0:T(8,128)(2,1)S(1)}, u32[]{:S(2)}, u32[]{:S(2)}) async-start(bf16[4,64,1152]{2,1,0:T(8,128)(2,1)} %get-tuple-element.26), calls=%async_computation | async-start | bytes 1179648 | tf_op jit(solution)/shard_map/all_to_all | solution.py:642
  74.9 27.6 %all-to-all-start.3 = ((f32[64,1,128]{2,1,0:T(1,128)}), f32[64,1,128]{2,1,0:T(1,128)S(1)}, u32[]{:S(2)}, u32[]{:S(2)}) async-start(f32[64,1,128]{2,1,0:T(1,128)} %bitcast.20), calls=%async_computation.3 | async-start | bytes 65536 | tf_op jit(solution)/shard_map/all_to_all | solution.py:663
  88.9 5.7 %collective-permute-start.1 = (f32[3,1280]{1,0:T(4,128)S(1)}, f32[3,1280]{1,0:T(4,128)S(1)}, u32[]{:S(2)}, u32[]{:S(2)}) collective-permute-start(f32[3,1280]{1,0:T(4,128)S(1)} %slice.11), channel_id=1, source_target_pairs={{8,0},{16,8},{24,16},{32,24},{40,32},{48,40},{56,48},{64,56},{72,6... | collective-permute-start | bytes 46088 | tf_op jit(solution)/shard_map/ppermute | solution.py:580
  94.6 0.6 copy-start

commit v6 on v5

--- a/solution.py
+++ b/solution.py
@@ -403,7 +403,7 @@
 
 
 def taps_kernel(
-    carry_hbm, lines_hbm, inside_hbm, bx_hbm, ady_hbm, marked_hbm, part_hbm, reach_hbm, weight_hbm, meets_hbm, sides_hbm,
+    order, carry_hbm, lines_hbm, inside_hbm, bx_hbm, ady_hbm, marked_hbm, part_hbm, reach_hbm, weight_hbm, meets_hbm, sides_hbm,
     base_hbm,
     head_ref, terms_ref,
     carry_ref, lines_ref, inside_ref, bx_ref, ady_ref, marked_ref, part_ref, reach_ref, weight_ref, meets_ref,
@@ -492,19 +492,18 @@
         sums_ref[:, tile * 128 : tile * 128 + 128] = jnp.zeros((8, 128), F32)
     aside = pltpu.roll(sums_ref[...], 0, 1, stride=width // 2, stride_axis=0)
     sums_ref[...] = pltpu.roll(aside, 0, 1, stride=width - width // 2, stride_axis=0)
-    for target in range(targets):
+    for place, target in enumerate(order):
         tile, at = divmod(target * width, 128)
         part = sums_ref[:, tile * 128 : tile * 128 + 128]
         if at:
             part = jnp.where(lane >= at, part, sums_ref[:, tile * 128 + 128 : tile * 128 + 256])
             part = pltpu.roll(part, 128 - at, 1)
-        terms_ref[target : target + 1, :] = jnp.sum(jnp.where(own, part, 0.0), axis=0, keepdims=True)
+        terms_ref[place : place + 1, :] = jnp.sum(jnp.where(own, part, 0.0), axis=0, keepdims=True)
 
 
 def rest_kernel(
     carry_ref, marked_ref, bx_ref, ady_ref, part_ref, reach_ref, inside_ref, lines_ref, sums_ref, heads_ref, weight_ref,
-    back_ref,
-    out_ref, raw_out_ref, dpre, after,
+    out_ref, raw_out_ref, edge_ref, dpre,
 ):
     tokens, channels = part_ref.shape
     inner = bx_ref.shape[1]
@@ -540,8 +539,6 @@
         step, gate, rate = (heads_ref[i * heads : (i + 1) * heads, rows] for i in range(3))
         raw_out_ref[:, rows] = ((sums_ref[heads : 2 * heads, rows] + col_sum.T) / step + rate * dlog) * gate
     dpre[tokens : tokens + 8, :] = jnp.zeros((8, channels), F32)
-    after[...] = jnp.zeros((8, channels), F32)
-    after[8 - (KERNEL - 1) : 8, :] = back_ref[...]
     weight = weight_ref[...].astype(F32)
     for low in range(0, channels, 128):
         cols = slice(low, low + 128)
@@ -551,16 +548,25 @@
                 ahead = start + KERNEL - 1 - tap
                 total = total + dpre[ahead : ahead + 64, cols] * weight[tap : tap + 1, cols]
             if start == tokens - 64:
-                total = jnp.concatenate([total[0:56], total[56:64] + after[:, cols]], axis=0)
+                edge_ref[:, cols] = total[48:64]
             out_ref[start : start + 64, cols] = total.astype(BF16)
 
 
-def shares_kernel(scale, terms_ref, weight_ref, bias_ref):
+def shares_kernel(scale, terms_ref, edge_ref, back_ref, held_ref, weight_ref, bias_ref, out_hbm, last, sem):
+    rows = last.shape[0]
+    line = lax.broadcasted_iota(jnp.int32, last.shape, 0)
+    total = edge_ref[...]
+    for at in range(KERNEL - 1):
+        total = total + jnp.where(line == rows - (KERNEL - 1) + at, back_ref[at : at + 1, :], 0.0)
+    last[...] = total.astype(BF16)
+    copy = pltpu.make_async_copy(last, out_hbm.at[out_hbm.shape[0] - rows :], sem)
+    copy.start()
     total = jnp.sum(terms_ref[...], axis=0) * scale
     width = bias_ref.shape[1]
     for tap in range(KERNEL):
         weight_ref[tap, :, :] = total[:, tap * width : (tap + 1) * width]
     bias_ref[...] = total[:, KERNEL * width : (KERNEL + 1) * width]
+    copy.wait()
 
 
 def call(kernel, out_shape, scratch=(), flops=0, moved=0, vmem=WIDE, **specs):
@@ -653,28 +659,35 @@
 
     sources = (carry, lines, inside, bx, ady, marked, part, reach, conv_weight, meets, sides, base)
     tops = [shape((16,) + a.shape[1:], a.dtype) if a is marked or a is part or a is reach else a for a in sources]
+    order = [
+        dp * ctx_size + (place + ctx_size // 4) % ctx_size for dp in range(dp_size) for place in range(ctx_size)
+    ]
     head, terms = call(
-        taps_kernel,
+        lambda *refs: taps_kernel(order, *refs),
         (shape((8, channels), F32), shape((devices, 128), F32)),
         buffers(*tops) + [pltpu.VMEM((8, channels + 2 * 128), F32), pltpu.SemaphoreType.DMA((len(sources),))],
         in_specs=[placed] * len(sources),
     )(*sources)
 
-    terms = lax.all_to_all(terms.reshape(devices, 1, 128), ("dp",) + CTX, 0, 0, tiled=True)
+    terms = lax.all_to_all(terms.reshape(devices, 1, 128), ("dp",) + CTX, 0, 0, tiled=True, axis_index_groups=[order])
     back = shifted(head[: KERNEL - 1], CTX, -1)
-    out, grad_raw = call(
+    out, grad_raw, edge = call(
         rest_kernel,
-        (shape((tokens, channels), BF16), shape((heads, tokens), F32)),
-        [padded, pltpu.VMEM((8, channels), F32)],
+        (shape((tokens, channels), BF16), shape((heads, tokens), F32), shape((16, channels), F32)),
+        [padded],
         flops=10**9,
         moved=10**7,
-    )(carry, marked, bx, ady, part, reach, inside, lines, sums, per_head, conv_weight, back)
+    )(carry, marked, bx, ady, part, reach, inside, lines, sums, per_head, conv_weight)
     width = channels // devices
-    grad_weight, grad_bias = call(
+    grad_weight, grad_bias, out = call(
         lambda *refs: shares_kernel(1.0 / (dp_size * length), *refs),
-        (shape((KERNEL, 1, width), F32), shape((1, width), F32)),
+        (shape((KERNEL, 1, width), F32), shape((1, width), F32), shape((tokens, channels), BF16)),
+        [pltpu.VMEM((16, channels), BF16), pltpu.SemaphoreType.DMA],
         vmem=NARROW,
-    )(terms)
+        in_specs=[held, held, held, placed],
+        out_specs=(held, held, placed),
+        input_output_aliases={3: 2},
+    )(terms, edge, back, out)
     return (out[None], grad_raw.T[None], grad_weight, grad_bias)
 
 

time: 104 us -> 103 us (level)
  waiting for transfers between devices: 8.75 us -> 4.7 us
  starting transfers between devices: 26.2 us -> 28.4 us
    ppermute x2, waiting for transfers between devices: 4.27 us -> 0.08 us  [shifted(): return lax.ppermute(value, axis, pairs)]
    all_to_all x1, starting transfers between devices: 13.2 us -> 15.4 us  [body(): lax.all_to_all(terms.reshape(devices, 1, 128), ('dp',) + CTX, 0, 0, tiled...]
  transfers between devices with their start and end apart: 4 -> 4, of which waited for: 4 -> 3; matrix products, arithmetic and copies ran while one was open for 2% -> 2% of each run, Pallas kernels for 15% -> 15%
where the time goes in v6:
time: 103 us; the launch traced here: 102 us
  blocking collectives  37.7 us (37%)
  starting transfers between devices  28.4 us (28%)
  Pallas kernels  26.6 us (26%)
  waiting for transfers between devices  4.7 us (5%)
  local copies, waits for them, and re-layouts  4.3 us (4%)
    all_to_all x1, blocking collectives, body(): lax.all_to_all(totals, 'ch', 0, 0, tiled=True, axis_index_groups=turned)  25.5 us
    all_to_all x1, starting transfers between devices, body(): lax.all_to_all(terms.reshape(devices, 1, 128), ('dp',) + CTX, 0, 0, tiled...  15.4 us
    all_to_all x1, blocking collectives, body(): lax.all_to_all(states, 'cl', 0, 0, tiled=True, axis_index_groups=[list(NE...  12.2 us
    pallas_call x1, Pallas kernels, body(): call(lambda *refs: local_kernel(length, *refs), (shape((tokens, channels)...  9.44 us
    all_to_all x1, starting transfers between devices, body(): lax.all_to_all(pack, 'cl', 0, 0, tiled=True, axis_index_groups=[list(NEAR)])  7.68 us
    pallas_call x1, Pallas kernels, body(): call(rest_kernel, (shape((tokens, channels), BF16), shape((heads, tokens)...  6.36 us
    ppermute x2, starting transfers between devices, shifted(): return lax.ppermute(value, axis, pairs)  5.27 us
    pallas_call x1, Pallas kernels, body(): call(lambda *refs: front_kernel(length, *refs), results, buffers(*sources...  4.83 us
  transfers between devices with their start and end apart: 4, of which 3 were waited for; matrix products, arithmetic and copies ran while one was open for 2% of the time, Pallas kernels for 15%

profile of v6, /device:TPU:24, one launch (start us, length us, event | category | flops | bytes accessed | tf_op | source)
XLA Modules:
  0.0 102.5 jit_solution(11956705978218519834)
XLA Ops:
  0.6 0.7 slice_bitcast_fusion
  1.4 3.8 %collective-permute-start = (bf16[3,1280]{1,0:T(4,128)(2,1)S(1)}, bf16[3,1280]{1,0:T(4,128)(2,1)S(1)}, u32[]{:S(2)}, u32[]{:S(2)}) collective-permute-start(bf16[3,1280]{1,0:T(4,128)(2,1)S(1)} %slice_bitcast_fusion), channel_id=1, source_target_pairs={{0,8},{8,16},{16,24},{24,32},{32,40},{40,48},{48,56},{56,64},{64,7... | collective-permute-start | bytes 23048 | tf_op jit(solution)/shard_map/ppermute | solution.py:586
  5.2 1.3 %broadcast_in_dim.20.refs_8_.refs_9_ = f32[1,1280]{1,0:T(1,128)} reshape(f32[1280]{0:T(1024)} %param.14) | data formatting | bytes 10240 | tf_op jit(solution)/shard_map/broadcast_in_dim | solution.py:609
  6.5 0.1 collective-permute-done.refs_1_
  6.6 0.0 copy-start.1
  6.6 0.6 copy-done.1
  7.2 4.8 %shard_map.120 = (bf16[256,1280]{1,0:T(8,128)(2,1)}, bf16[256,1024]{1,0:T(8,128)(2,1)}, bf16[256,1024]{1,0:T(8,128)(2,1)}, bf16[4,64,1152]{2,1,0:T(8,128)(2,1)}) custom-call(bf16[256,1280]{1,0:T(8,128)(2,1)} %bitcast.16, bf16[3,1280]{1,0:T(4,128)(2,1)} %copy-done.1, bf16[256,1024]{1,0:T(8,128)(2,1)} %bitcast.19, f32[16,256]{1,0:T(8,128)} %bitcast.22, ...), custom_call_target="tpu_custom_call" | custom-call | tf_op jit(solution)/shard_map/pallas_call | solution.py:621
  12.0 7.7 %all-to-all-start = ((bf16[4,64,1152]{2,1,0:T(8,128)(2,1)}), bf16[4,64,1152]{2,1,0:T(8,128)(2,1)S(1)}, u32[]{:S(2)}, u32[]{:S(2)}) async-start(bf16[4,64,1152]{2,1,0:T(8,128)(2,1)} %get-tuple-element.28), calls=%async_computation | async-start | bytes 1179648 | tf_op jit(solution)/shard_map/all_to_all | solution.py:648
  19.7 9.4 %shard_map.121 = (f32[256,1280]{1,0:T(8,128)}, f32[256,1280]{1,0:T(8,128)}, f32[32,256]{1,0:T(8,128)}, f32[48,256]{1,0:T(8,128)}, bf16[256,256]{1,0:T(8,128)(2,1...) custom-call(bf16[256,1280]{1,0:T(8,128)(2,1)} %bitcast.17, ...), custom_call_target="tpu_custom_call" | custom-call | flops 1000000000 | bytes 10000000 | tf_op jit(solution)/shard_map/pallas_call | solution.py:629
  29.1 3.5 %all-to-all-done.near_ref = bf16[4,64,1152]{2,1,0:T(8,128)(2,1)S(1)} async-done(((bf16[4,64,1152]{2,1,0:T(8,128)(2,1)}), bf16[4,64,1152]{2,1,0:T(8,128)(2,1)S(1)}, u32[]{:S(2)}, u32[]{:S(2)}) %all-to-all-start) | async-done | bytes 589856 | tf_op jit(solution)/shard_map/all_to_all | solution.py:648
  32.6 0.4 shard_map.122
  33.0 25.5 %all_to_all.20.far_ref = bf16[4,32,1152]{2,1,0:T(8,128)(2,1)S(1)} all-to-all(bf16[4,32,1152]{2,1,0:T(8,128)(2,1)S(1)} %shard_map.122), channel_id=1, replica_groups={{64,96,0,32},{65,97,1,33},{66,98,2,34},{67,99,3,35},{68,100,4,36},{69,1..., dimensions={0} | all-to-all | bytes 589824 | tf_op jit(solution)/shard_map/all_to_all | solution.py:652
  58.5 0.6 shard_map.123
  59.0 12.2 %all_to_all.21.refs_0_.carry_ref = bf16[4,64,1024]{2,1,0:T(8,128)(2,1)} all-to-all(bf16[4,64,1024]{2,1,0:T(8,128)(2,1)S(1)} %shard_map.123), channel_id=1, replica_groups={{16,8,0,24},{17,9,1,25},{18,10,2,26},{19,11,3,27},{20,12,4,28},{21,13,5..., dimensions={0} | all-to-all | bytes 1048576 | tf_op jit(solution)/shard_map/all_to_all | solution.py:658
  71.2 3.7 %shard_map.124 = (f32[8,1280]{1,0:T(8,128)}, f32[64,128]{1,0:T(8,128)}) custom-call(bf16[4,64,1024]{2,1,0:T(8,128)(2,1)} %all_to_all.21.refs_0_.carry_ref, f32[8,1024]{1,0:T(8,128)} %get-tuple-element.34.refs_1_.lines_ref, f32[2,128,1024]{2,1,0:T(8,128)} %get-tuple-element.35.refs_2_.inside_ref, bf16[256,1024]{1,0:T(8,128)(2,1)} %get-tuple-element.30.refs_11_.refs_3_.bx_ref, ...), custom_call_target="tpu_custom_call" | custom-call | tf_op jit(solution)/shard_map/pallas_call | solution.py:665
  74.9 15.4 %all-to-all-start.3 = ((f32[64,1,128]{2,1,0:T(1,128)}), f32[64,1,128]{2,1,0:T(1,128)S(1)}, u32[]{:S(2)}, u32[]{:S(2)}) async-start(f32[64,1,128]{2,1,0:T(1,128)} %bitcast.21), calls=%async_computation.3 | async-start | bytes 65536 | tf_op jit(solution)/shard_map/all_to_all | solution.py:672
  90.4 0.8 slice.11
  91.1 1.5 %collective-permute-start.1 = (f32[3,1280]{1,0:T(4,128)S(1)}, f32[3,1280]{1,0:T(4,128)S(1)}, u32[]{:S(2)}, u32[]{:S(2)}) collective-permute-start(f32[3,1280]{1,0:T(4,128)S(1)} %slice.11), channel_id=1, source_target_pairs={{8,0},{16,8},{24,16},{32,24},{40,32},{48,40},{56,48},{64,56},{72,6... | collective-permute-start | bytes 46088 | tf_op jit(solution)/shard_map/ppermute | solution.py:586
  92.6 6.4 %shard_map.125 = (bf16[256,1280]{1,0:T(8,128)(2,1)}, f32[16,256]{1,0:T(8,128)}, f32[16,1280]{1,0:T(8,128)}) custom-call(bf16[4,64,1024]{2,1,0:T(8,128)(2,1)} %all_to_all.21.refs_0_.carry_ref, bf16[256,256]{1,0:T(8,128)(2,1)} %get-tuple-element.36.refs_5_.marked_ref, bf16[256,1024]{1,0:T(8,128)(2,1)} %get-tuple-element.30.refs_11_.refs_3_.bx_ref, ...), custom_call_target="tpu_custom_call" | custom-call | flops 1000000000 | bytes 10000000 | tf_op jit(solution)/shard_map/pallas_call | solution.py:674
  99.0 0.0 collective-permute-done.1.refs_2_
  99.0 1.2 %all-to-all-done.3.refs_0_ = f32[64,1,128]{2,1,0:T(1,128)S(1)} async-done(((f32[64,1,128]{2,1,0:T(1,128)}), f32[64,1,128]{2,1,0:T(1,128)S(1)}, u32[]{:S(2)}, u32[]{:S(2)}) %all-to-all-start.3) | async-done | bytes 32800 | tf_op jit(solution)/shard_map/all_to_all | solution.py:672
  100.1 0.0 copy-start
  100.1 0.9 copy-done
  101.0 1.3 %shard_map.126 = (f32[4,1,20]{2,1,0:T(1,128)}, f32[1,20]{1,0:T(1,128)}, bf16[256,1280]{1,0:T(8,128)(2,1)}) custom-call(f32[64,1,128]{2,1,0:T(1,128)S(1)} %all-to-all-done.3.refs_0_, f32[16,1280]{1,0:T(8,128)S(1)} %copy-done, f32[3,1280]{1,0:T(4,128)S(1)} %collective-permute-done.1.refs_2_, ...), custom_call_target="tpu_custom_call", output_to_operand_aliasing={{2}: (3, {})} | custom-call | tf_op jit(solution)/shard_map/pallas_call | solution.py:682
Async XLA Ops:
  1.4 5.2 %collective-permute-start = (bf16[3,1280]{1,0:T(4,128)(2,1)S(1)}, bf16[3,1280]{1,0:T(4,128)(2,1)S(1)}, u32[]{:S(2)}, u32[]{:S(2)}) collective-permute-start(bf16[3,1280]{1,0:T(4,128)(2,1)S(1)} %slice_bitcast_fusion), channel_id=1, source_target_pairs={{0,8},{8,16},{16,24},{24,32},{32,40},{40,48},{48,56},{56,64},{64,7... | collective-permute-start | bytes 23048 | tf_op jit(solution)/shard_map/ppermute | solution.py:586
  6.6 0.6 copy-start.1
  12.0 20.6 %all-to-all-start = ((bf16[4,64,1152]{2,1,0:T(8,128)(2,1)}), bf16[4,64,1152]{2,1,0:T(8,128)(2,1)S(1)}, u32[]{:S(2)}, u32[]{:S(2)}) async-start(bf16[4,64,1152]{2,1,0:T(8,128)(2,1)} %get-tuple-element.28), calls=%async_computation | async-start | bytes 1179648 | tf_op jit(solution)/shard_map/all_to_all | solution.py:648
  74.9 25.2 %all-to-all-start.3 = ((f32[64,1,128]{2,1,0:T(1,128)}), f32[64,1,128]{2,1,0:T(1,128)S(1)}, u32[]{:S(2)}, u32[]{:S(2)}) async-start(f32[64,1,128]{2,1,0:T(1,128)} %bitcast.21), calls=%async_computation.3 | async-start | bytes 65536 | tf_op jit(solution)/shard_map/all_to_all | solution.py:672
  91.1 7.8 %collective-permute-start.1 = (f32[3,1280]{1,0:T(4,128)S(1)}, f32[3,1280]{1,0:T(4,128)S(1)}, u32[]{:S(2)}, u32[]{:S(2)}) collective-permute-start(f32[3,1280]{1,0:T(4,128)S(1)} %slice.11), channel_id=1, source_target_pairs={{8,0},{16,8},{24,16},{32,24},{40,32},{48,40},{56,48},{64,56},{72,6... | collective-permute-start | bytes 46088 | tf_op jit(solution)/shard_map/ppermute | solution.py:586
  100.1 0.9 copy-start
